TPU v7x, 32 devices: a whole 2x2x4 slice. The times are simulated.
32 devices in a mesh: rows: 8 (over z, x), cols: 4 (over y, core).
Axes of the slice: x: 2, y: 2, z: 4, core: 2. Of those that a mesh axis runs over, the one named last changes fastest.
Arguments:
- row_master: float32 [32, 1024, 256], P(None, ('rows', 'cols')), may hold values from -1.5 to 1.5
- row_accum: float32 [32, 1024, 256], P(None, ('rows', 'cols')), may hold values from 0.5 to 8
- col_master: float32 [32, 1024, 256], P(None, ('rows', 'cols')), may hold values from -1.5 to 1.5
- col_accum: float32 [32, 1024, 256], P(None, ('rows', 'cols')), may hold values from 0.5 to 8
- pairs: int32 [96, 2], P(('rows', 'cols')), may hold values from 0 to 31
- live: int32 [32], P(('rows', 'cols')), may hold values from 1 to 3, as said below
- counts: int32 [96, 1024, 1024], P(('rows', 'cols')), may hold values from 0 to 961
- row_marginal: int32 [32, 1024], replicated, may hold values from 1000 to 30000
- col_marginal: int32 [32, 1024], replicated, may hold values from 1000 to 30000
Outputs:
- row_new: float32 [32, 1024, 256], P(None, ('rows', 'cols'))
- row_accum_new: float32 [32, 1024, 256], P(None, ('rows', 'cols'))
- col_new: float32 [32, 1024, 256], P(None, ('rows', 'cols'))
- col_accum_new: float32 [32, 1024, 256], P(None, ('rows', 'cols'))
Inputs may be any that keep to these rules, and one draw needn't show every extreme that they name: `live`: at least one device works on its whole list and at least one on a single pair.
All inputs are finite; a program needn't handle non-finite values.
Results may differ from a plain program's by a relative error of at most 0.0048.
Values may be sent and summed in bfloat16 or wider, within the bound.
No kernel may reach another device: no remote copies, remote signals or barrier semaphores. Data moves between devices by JAX's collectives and lax.ppermute only.
A program may use at most 128 MiB of HBM per device.

v0:
```python
import jax
import jax.numpy as jnp
from jax import lax
from jax.sharding import PartitionSpec as P

LOG_TOTAL = 14.3
LEARN_RATE = 0.05


def slot_delta(rows_blk, cols_blk, count, row_count, col_count):
    logits = lax.dot_general(
        rows_blk, cols_blk, (((1,), (1,)), ((), ())), preferred_element_type=jnp.float32
    )
    counts_f = count.astype(jnp.float32)
    target = jnp.log(jnp.maximum(counts_f, 1.0)) + LOG_TOTAL
    target = (
        target
        - jnp.log(row_count.astype(jnp.float32))[:, None]
        - jnp.log(col_count.astype(jnp.float32))[None, :]
    )
    spread = logits - target
    weight = 0.1 + 0.25 * jnp.sqrt(counts_f)
    grad = jnp.where(counts_f > 0.0, weight * spread, jax.nn.sigmoid(spread))
    return grad * (1.0 / jnp.sqrt(jnp.float32(count.shape[1])))


def block_grads(rows_blk, cols_blk, delta):
    row_part = jnp.dot(delta, cols_blk, preferred_element_type=jnp.float32)
    col_part = lax.dot_general(
        delta, rows_blk, (((0,), (0,)), ((), ())), preferred_element_type=jnp.float32
    )
    return (row_part, col_part)


def adagrad(master, accum, grad):
    accum_new = accum + grad * grad
    return (master - LEARN_RATE * grad / jnp.sqrt(accum_new), accum_new)


def collect(ids, returned, blocks):
    onehot = (ids.reshape(-1)[None, :] == jnp.arange(blocks, dtype=jnp.int32)[:, None]).astype(
        jnp.float32
    )
    flat = returned.reshape(
        returned.shape[0] * returned.shape[1], returned.shape[2] * returned.shape[3]
    )
    summed = jnp.dot(
        onehot, flat, precision=lax.Precision.HIGHEST, preferred_element_type=jnp.float32
    )
    return summed.reshape(blocks, returned.shape[2], returned.shape[3])


def body(
    row_master, row_accum, col_master, col_accum, pairs, live, counts, row_marginal, col_marginal
):
    slots = pairs.shape[0]
    blocks = row_master.shape[0]
    piece = row_master.shape[1]
    width = row_master.shape[2]
    nodes = lax.axis_size(("rows", "cols"))
    requests = lax.all_gather(pairs, ("rows", "cols"), axis=0, tiled=True).reshape(nodes, slots, 2)
    row_ids = requests[:, :, 0].T
    col_ids = requests[:, :, 1].T
    send_rows = row_master.astype(jnp.bfloat16)[row_ids]
    send_cols = col_master.astype(jnp.bfloat16)[col_ids]
    got_rows, got_cols = (
        lax.all_to_all(send_rows, ("rows", "cols"), split_axis=1, concat_axis=1, tiled=True),
        lax.all_to_all(send_cols, ("rows", "cols"), split_axis=1, concat_axis=1, tiled=True),
    )
    got_rows = got_rows.reshape(slots, nodes * piece, width)
    got_cols = got_cols.reshape(slots, nodes * piece, width)
    own_live = live[0]
    row_parts = []
    col_parts = []
    for slot in range(slots):
        rows_blk = got_rows[slot]
        cols_blk = got_cols[slot]
        row_count = row_marginal[pairs[slot, 0]]
        col_count = col_marginal[pairs[slot, 1]]
        delta = slot_delta(rows_blk, cols_blk, counts[slot], row_count, col_count)
        delta = jnp.where(slot < own_live, delta, 0.0).astype(jnp.bfloat16)
        row_part, col_part = block_grads(rows_blk, cols_blk, delta)
        row_parts.append(row_part)
        col_parts.append(col_part)
    back_rows = jnp.stack(row_parts)
    back_cols = jnp.stack(col_parts)
    ret_rows, ret_cols = (
        lax.all_to_all(
            back_rows.reshape(slots, nodes, piece, width),
            ("rows", "cols"),
            split_axis=1,
            concat_axis=1,
            tiled=True,
        ),
        lax.all_to_all(
            back_cols.reshape(slots, nodes, piece, width),
            ("rows", "cols"),
            split_axis=1,
            concat_axis=1,
            tiled=True,
        ),
    )
    row_grad = collect(row_ids, ret_rows, blocks)
    col_grad = collect(col_ids, ret_cols, blocks)
    row_new, row_accum_new = adagrad(row_master, row_accum, row_grad)
    col_new, col_accum_new = adagrad(col_master, col_accum, col_grad)
    return (row_new, row_accum_new, col_new, col_accum_new)


def solution(mesh):
    return jax.shard_map(
        body,
        mesh=mesh,
        in_specs=(
            P(None, ("rows", "cols"), None),
            P(None, ("rows", "cols"), None),
            P(None, ("rows", "cols"), None),
            P(None, ("rows", "cols"), None),
            P(("rows", "cols"), None),
            P(("rows", "cols")),
            P(("rows", "cols"), None, None),
            P(),
            P(),
        ),
        out_specs=(
            P(None, ("rows", "cols"), None),
            P(None, ("rows", "cols"), None),
            P(None, ("rows", "cols"), None),
            P(None, ("rows", "cols"), None),
        ),
        check_vma=False,
    )
```

profile of v0, /device:TPU:0, one launch (start us, length us, event | category | flops | bytes accessed | tf_op | source)
XLA Modules:
  0.0 312.4 jit_solution(15899833091329600351)
XLA Ops:
  0.6 43.5 %all-gather = s32[32,3,2]{1,2,0:T(2,128)S(1)} all-gather(s32[1,3,2]{1,2,0:T(2,128)} %bitcast.214), channel_id=1, replica_groups=mesh['rows'=8,'cols'=4] {'rows','cols'}, dimensions={0}, use_global_device_ids=true | all-gather | bytes 792 | tf_op jit(solution)/shard_map/all_gather | solution.py:61
  47.7 2.7 all-to-all-start.1
  50.6 1.9 gather_fusion
  52.5 2.7 copy.59
  55.2 32.7 %all-to-all-done.1 = bf16[3,32,32,256]{3,2,0,1:T(8,128)(2,1)S(1)} async-done(((bf16[3,32,32,256]{3,2,0,1:T(8,128)(2,1)}), bf16[3,32,32,256]{3,2,0,1:T(8,128)(2,1)S(1)}, u32[]{:S(2)}, u32[]{:S(2)}) %all-to-all-start.1) | async-done | bytes 1572896 | tf_op jit(solution)/shard_map/all_to_all | solution.py:68
  87.9 3.7 %all-to-all-start = ((bf16[3,32,32,256]{3,2,0,1:T(8,128)(2,1)}), bf16[3,32,32,256]{3,2,0,1:T(8,128)(2,1)}, u32[]{:S(2)}, u32[]{:S(2)}) async-start(bf16[3,32,32,256]{3,2,0,1:T(8,128)(2,1)} %copy.59), calls=%async_computation | async-start | bytes 3145728 | tf_op jit(solution)/shard_map/all_to_all | solution.py:67
  106.3 22.9 %all-to-all-done = bf16[3,32,32,256]{3,2,0,1:T(8,128)(2,1)} async-done(((bf16[3,32,32,256]{3,2,0,1:T(8,128)(2,1)}), bf16[3,32,32,256]{3,2,0,1:T(8,128)(2,1)}, u32[]{:S(2)}, u32[]{:S(2)}) %all-to-all-start) | async-done | bytes 1572896 | tf_op jit(solution)/shard_map/all_to_all | solution.py:67
  130.9 6.2 %fusion.11 = bf16[1024,1024]{1,0:T(8,128)(2,1)S(1)} fusion(s32[3,1024,1024]{2,1,0:T(8,128)} %param.15, bf16[1024,256]{1,0:T(8,128)(2,1)S(1)} %bitcast.200, bf16[1024,256]{1,0:T(8,128)(2,1)S(1)} %bitcast.210, f32[1024]{0:T(1024)S(1)} %bitcast.220, f32[1024]{0:T(1024)S(1)} %bitcast.218, pred[]{:T(512)} %bitcast.23), kind=kOutput, calls=%fused_computation.17 | convolution fusion | flops 554696704 | bytes 7348225 | tf_op jit(solution)/shard_map/dot_general | solution.py:11
  137.8 4.1 %fusion.5 = bf16[1024,1024]{1,0:T(8,128)(2,1)S(1)} fusion(s32[3,1024,1024]{2,1,0:T(8,128)S(1)} %bitcast.222, bf16[1024,256]{1,0:T(8,128)(2,1)S(1)} %bitcast.202, bf16[1024,256]{1,0:T(8,128)(2,1)S(1)} %bitcast.208, f32[1024]{0:T(1024)S(1)} %bitcast.219, f32[1024]{0:T(1024)S(1)} %bitcast.217, pred[]{:T(512)} %bitcast.36), kind=kOutput, calls=%fused_computation.9 | convolution fusion | flops 554696704 | bytes 7348225 | tf_op jit(solution)/shard_map/dot_general | solution.py:11
  142.7 4.1 %fusion.17 = bf16[1024,1024]{1,0:T(8,128)(2,1)S(1)} fusion(s32[3,1024,1024]{2,1,0:T(8,128)S(1)} %bitcast.222, bf16[1024,256]{1,0:T(8,128)(2,1)S(1)} %bitcast.204, bf16[1024,256]{1,0:T(8,128)(2,1)S(1)} %bitcast.206, f32[1024]{0:T(1024)S(1)} %bitcast.216, f32[1024]{0:T(1024)S(1)} %bitcast.215, pred[]{:T(512)} %bitcast.4), kind=kOutput, calls=%fused_computation.25 | convolution fusion | flops 554696704 | bytes 7348225 | tf_op jit(solution)/shard_map/dot_general | solution.py:11
  149.1 2.0 copy.62
  151.0 3.8 %all-to-all-start.2 = ((f32[3,32,32,256]{3,2,0,1:T(8,128)}), f32[3,32,32,256]{3,2,0,1:T(8,128)S(1)}, u32[]{:S(2)}, u32[]{:S(2)}) async-start(f32[3,32,32,256]{3,2,0,1:T(8,128)} %copy.62), calls=%async_computation.2 | async-start | bytes 6291456 | tf_op jit(solution)/shard_map/all_to_all | solution.py:88
  154.9 3.9 %copy.67 = bf16[1024,1024]{1,0:T(8,128)(2,1)} copy(bf16[1024,1024]{0,1:T(8,128)(2,1)} %bitcast.194) | data formatting | bytes 4194304 | tf_op jit(solution)/shard_map/dot_general | solution.py:29
  158.8 3.9 %copy.69 = bf16[1024,1024]{1,0:T(8,128)(2,1)} copy(bf16[1024,1024]{0,1:T(8,128)(2,1)} %bitcast.192) | data formatting | bytes 4194304 | tf_op jit(solution)/shard_map/dot_general | solution.py:29
  162.7 3.9 %copy.68 = bf16[1024,1024]{1,0:T(8,128)(2,1)} copy(bf16[1024,1024]{0,1:T(8,128)(2,1)} %bitcast.190) | data formatting | bytes 4194304 | tf_op jit(solution)/shard_map/dot_general | solution.py:29
  166.7 2.5 convolution_bitcast_fusion.2
  169.2 2.4 convolution_bitcast_fusion
  172.8 2.1 copy.70
  174.8 51.6 %all-to-all-done.2 = f32[3,32,32,256]{3,2,0,1:T(8,128)S(1)} async-done(((f32[3,32,32,256]{3,2,0,1:T(8,128)}), f32[3,32,32,256]{3,2,0,1:T(8,128)S(1)}, u32[]{:S(2)}, u32[]{:S(2)}) %all-to-all-start.2) | async-done | bytes 3145760 | tf_op jit(solution)/shard_map/all_to_all | solution.py:88
  226.4 4.6 %all-to-all-start.3 = ((f32[3,32,32,256]{3,2,0,1:T(8,128)}), f32[3,32,32,256]{3,2,0,1:T(8,128)}, u32[]{:S(2)}, u32[]{:S(2)}) async-start(f32[3,32,32,256]{3,2,0,1:T(8,128)} %copy.70), calls=%async_computation.3 | async-start | bytes 6291456 | tf_op jit(solution)/shard_map/all_to_all | solution.py:95
  232.8 4.2 %copy_subtract_fusion.1 = (f32[32,32,256]{2,0,1:T(8,128)S(1)}, f32[32,32,256]{2,0,1:T(8,128)S(1)}) fusion(f32[32,32,256]{2,1,0:T(8,128)S(1)} %copy-done.5, f32[32,32,256]{2,1,0:T(8,128)S(1)} %copy-done.11, s32[96]{0:T(128)S(1)} %eq.30, f32[12,8,32,256]{3,2,1,0:T(8,128)S(1)} %bitcast.187), kind=kOutput, calls=%fused_computation.48 | convolution fusion | flops 303303680 | bytes 7340416 | tf_op jit(solution)/shard_map/dot_general | solution.py:47
  240.1 62.7 %all-to-all-done.3 = f32[3,32,32,256]{3,2,0,1:T(8,128)} async-done(((f32[3,32,32,256]{3,2,0,1:T(8,128)}), f32[3,32,32,256]{3,2,0,1:T(8,128)}, u32[]{:S(2)}, u32[]{:S(2)}) %all-to-all-start.3) | async-done | bytes 3145760 | tf_op jit(solution)/shard_map/all_to_all | solution.py:95
  302.8 2.3 copy.71
  305.1 4.2 %copy_subtract_fusion = (f32[32,32,256]{2,0,1:T(8,128)S(1)}, f32[32,32,256]{2,0,1:T(8,128)S(1)}) fusion(f32[32,32,256]{2,1,0:T(8,128)S(1)} %copy-done.6, f32[32,32,256]{2,1,0:T(8,128)S(1)} %copy-done.12, s32[96]{0:T(128)S(1)} %eq.34, f32[12,8,32,256]{3,2,1,0:T(8,128)S(1)} %bitcast.188), kind=kOutput, calls=%fused_computation.46 | convolution fusion | flops 303303680 | bytes 7340416 | tf_op jit(solution)/shard_map/dot_general | solution.py:47
  (65 shorter events, 20.7 us)
Async XLA Ops:
  45.7 4.8 %copy-start.4 = (f32[32,32,256]{2,1,0:T(8,128)S(1)}, f32[32,32,256]{2,1,0:T(8,128)}, u32[]{:S(2)}) copy-start(f32[32,32,256]{2,1,0:T(8,128)} %param.9) | copy-start | bytes 3145732
  47.7 40.2 %all-to-all-start.1 = ((bf16[3,32,32,256]{3,2,0,1:T(8,128)(2,1)}), bf16[3,32,32,256]{3,2,0,1:T(8,128)(2,1)S(1)}, u32[]{:S(2)}, u32[]{:S(2)}) async-start(bf16[3,32,32,256]{3,2,0,1:T(8,128)(2,1)} %copy.61), calls=%async_computation.1 | async-start | bytes 3145728 | tf_op jit(solution)/shard_map/all_to_all | solution.py:68
  50.6 41.0 %copy-start.13 = (s32[3,2]{0,1:T(2,128)S(1)}, s32[3,2]{0,1:T(2,128)}, u32[]{:S(2)}) copy-start(s32[3,2]{0,1:T(2,128)} %param.13) | copy-start | bytes 76
  87.9 41.2 %all-to-all-start = ((bf16[3,32,32,256]{3,2,0,1:T(8,128)(2,1)}), bf16[3,32,32,256]{3,2,0,1:T(8,128)(2,1)}, u32[]{:S(2)}, u32[]{:S(2)}) async-start(bf16[3,32,32,256]{3,2,0,1:T(8,128)(2,1)} %copy.59), calls=%async_computation | async-start | bytes 3145728 | tf_op jit(solution)/shard_map/all_to_all | solution.py:67
  129.2 8.6 %slice-start = ((s8[12582912]{0:T(1024)(128)(4,1)}), s8[4194304]{0:T(1024)(128)(4,1)S(1)}, s32[]{:S(2)}) async-start(s8[12582912]{0:T(1024)(128)(4,1)} %bitcast.221), calls=%async_computation.4 | async-start | bytes 8388608
  130.8 6.2 %copy-start.7 = (bf16[1,32,32,256]{3,2,0,1:T(8,128)(2,1)}, bf16[1,32,32,256]{3,2,0,1:T(8,128)(2,1)S(1)}, u32[]{:S(2)}) copy-start(bf16[1,32,32,256]{3,2,0,1:T(8,128)(2,1)S(1)} %get-tuple-element.29) | copy-start | bytes 1572868
  130.8 7.0 %copy-start.9 = (bf16[1,32,32,256]{3,2,0,1:T(8,128)(2,1)}, bf16[1,32,32,256]{3,2,0,1:T(8,128)(2,1)S(1)}, u32[]{:S(2)}) copy-start(bf16[1,32,32,256]{3,2,0,1:T(8,128)(2,1)S(1)} %get-tuple-element.28) | copy-start | bytes 1572868
  130.8 11.8 %copy-start.10 = (bf16[1,32,32,256]{3,2,0,1:T(8,128)(2,1)}, bf16[1,32,32,256]{3,2,0,1:T(8,128)(2,1)S(1)}, u32[]{:S(2)}) copy-start(bf16[1,32,32,256]{3,2,0,1:T(8,128)(2,1)S(1)} %get-tuple-element.27) | copy-start | bytes 1572868
  130.8 7.0 %slice-start.1 = ((s8[12582912]{0:T(1024)(128)(4,1)}), s8[4194304]{0:T(1024)(128)(4,1)S(1)}, s32[]{:S(2)}) async-start(s8[12582912]{0:T(1024)(128)(4,1)} %bitcast.221), calls=%async_computation.5 | async-start | bytes 8388608
  130.9 7.0 %slice-start.2 = ((s8[12582912]{0:T(1024)(128)(4,1)}), s8[4194304]{0:T(1024)(128)(4,1)S(1)}, s32[]{:S(2)}) async-start(s8[12582912]{0:T(1024)(128)(4,1)} %bitcast.221), calls=%async_computation.6 | async-start | bytes 8388608
  137.0 4.9 %copy-start = (bf16[1024,1024]{1,0:T(8,128)(2,1)}, bf16[1024,1024]{1,0:T(8,128)(2,1)S(1)}, u32[]{:S(2)}) copy-start(bf16[1024,1024]{1,0:T(8,128)(2,1)S(1)} %fusion.11) | copy-start | bytes 6291460
  141.9 4.8 %copy-start.1 = (bf16[1024,1024]{1,0:T(8,128)(2,1)}, bf16[1024,1024]{1,0:T(8,128)(2,1)S(1)}, u32[]{:S(2)}) copy-start(bf16[1024,1024]{1,0:T(8,128)(2,1)S(1)} %fusion.5) | copy-start | bytes 6291460
  146.8 1.3 copy-start.2
  151.0 75.4 %all-to-all-start.2 = ((f32[3,32,32,256]{3,2,0,1:T(8,128)}), f32[3,32,32,256]{3,2,0,1:T(8,128)S(1)}, u32[]{:S(2)}, u32[]{:S(2)}) async-start(f32[3,32,32,256]{3,2,0,1:T(8,128)} %copy.62), calls=%async_computation.2 | async-start | bytes 6291456 | tf_op jit(solution)/shard_map/all_to_all | solution.py:88
  166.7 4.9 %copy-start.3 = (bf16[1024,1024]{1,0:T(8,128)(2,1)S(1)}, bf16[1024,1024]{1,0:T(8,128)(2,1)}, u32[]{:S(2)}) copy-start(bf16[1024,1024]{1,0:T(8,128)(2,1)} %copy.68) | copy-start | bytes 6291460
  166.7 5.0 %copy-start.8 = (bf16[1,32,32,256]{3,2,0,1:T(8,128)(2,1)S(1)}, bf16[1,32,32,256]{3,2,0,1:T(8,128)(2,1)}, u32[]{:S(2)}) copy-start(bf16[1,32,32,256]{3,2,0,1:T(8,128)(2,1)} %copy-done.7) | copy-start | bytes 1572868
  226.4 76.3 %all-to-all-start.3 = ((f32[3,32,32,256]{3,2,0,1:T(8,128)}), f32[3,32,32,256]{3,2,0,1:T(8,128)}, u32[]{:S(2)}, u32[]{:S(2)}) async-start(f32[3,32,32,256]{3,2,0,1:T(8,128)} %copy.70), calls=%async_computation.3 | async-start | bytes 6291456 | tf_op jit(solution)/shard_map/all_to_all | solution.py:95
  231.2 1.2 copy-start.5
  231.2 1.5 copy-start.11
  238.5 66.5 %copy-start.6 = (f32[32,32,256]{2,1,0:T(8,128)S(1)}, f32[32,32,256]{2,1,0:T(8,128)}, u32[]{:S(2)}) copy-start(f32[32,32,256]{2,1,0:T(8,128)} %param.11) | copy-start | bytes 3145732
  238.5 66.5 %copy-start.12 = (f32[32,32,256]{2,1,0:T(8,128)S(1)}, f32[32,32,256]{2,1,0:T(8,128)}, u32[]{:S(2)}) copy-start(f32[32,32,256]{2,1,0:T(8,128)} %param.12) | copy-start | bytes 3145732
where the time goes:
time: 313 us; the launch traced here: 312 us
  waiting for transfers between devices  170 us (54%)
  blocking collectives  43.5 us (14%)
  local copies, waits for them, and re-layouts  36.8 us (12%)
  matrix products  30.4 us (10%)
  starting transfers between devices  14.8 us (5%)
  between operations  13.2 us (4%)
  other arithmetic  3.69 us (1%)
    all_to_all x1, waiting for transfers between devices, body(): lax.all_to_all(back_cols.reshape(slots, nodes, piece, width), ('rows', 'c...  62.7 us
    all_to_all x1, waiting for transfers between devices, body(): lax.all_to_all(back_rows.reshape(slots, nodes, piece, width), ('rows', 'c...  51.6 us
    all_gather x1, blocking collectives, body(): lax.all_gather(pairs, ('rows', 'cols'), axis=0, tiled=True)  43.5 us
    all_to_all x1, waiting for transfers between devices, body(): lax.all_to_all(send_cols, ('rows', 'cols'), split_axis=1, concat_axis=1,...  32.7 us
    all_to_all x1, waiting for transfers between devices, body(): lax.all_to_all(send_rows, ('rows', 'cols'), split_axis=1, concat_axis=1,...  22.9 us
    dot_general x3, matrix products, slot_delta(): lax.dot_general(rows_blk, cols_blk, (((1,), (1,)), ((), ())), preferred_e...  14.3 us
    dot_general x3, local copies, waits for them, and re-layouts, block_grads(): lax.dot_general(delta, rows_blk, (((0,), (0,)), ((), ())), preferred_elem...  11.8 us
    unnamed x38, local copies, waits for them, and re-layouts  8.88 us
  transfers between devices with their start and end apart: 4, of which 4 were waited for; matrix products, arithmetic and copies ran while one was open for 11% of the time, Pallas kernels for 0%

commit v1 on v0

v1 whole, which is shorter than its diff:
```python
import functools

import jax
import jax.numpy as jnp
from jax import lax
from jax.experimental import pallas as pl
from jax.experimental.pallas import tpu as pltpu
from jax.sharding import PartitionSpec as P

LOG_TOTAL = 14.3
LEARN_RATE = 0.05
AXES = ("rows", "cols")
TILE = 256
VMEM_LIMIT = 48 * 1024 * 1024

BF16 = jnp.bfloat16
F32 = jnp.float32


def vmem_spec():
    return pl.BlockSpec(memory_space=pltpu.VMEM)


def params():
    return pltpu.CompilerParams(vmem_limit_bytes=VMEM_LIMIT)


def pick_kernel(first, count, req, row_ref, col_ref, out_ref):
    nodes = out_ref.shape[0]

    def one(node, carry):
        for k in range(count):
            a = req[node, 2 * (first + k)]
            b = req[node, 2 * (first + k) + 1]
            out_ref[node, 2 * k] = row_ref[a].astype(BF16)
            out_ref[node, 2 * k + 1] = col_ref[b].astype(BF16)
        return carry

    lax.fori_loop(0, nodes, one, 0)


def pick(req, row_master, col_master, first, count):
    nodes = req.shape[0]
    piece, width = row_master.shape[1:]
    out = jax.ShapeDtypeStruct((nodes, 2 * count, piece, width), BF16)
    return pl.pallas_call(
        functools.partial(pick_kernel, first, count),
        out_shape=out,
        grid_spec=pltpu.PrefetchScalarGridSpec(
            num_scalar_prefetch=1,
            in_specs=[vmem_spec(), vmem_spec()],
            out_specs=vmem_spec(),
            grid=(),
        ),
        compiler_params=params(),
        cost_estimate=pl.CostEstimate(
            flops=0,
            bytes_accessed=2 * row_master.size * 4 + nodes * 2 * count * piece * width * 2,
            transcendentals=0,
        ),
        name="pick",
    )(req, row_master, col_master)


def item_kernel(
    first, pairs, live, got_ref, counts_ref, rm_ref, cm_ref, out_ref, rows_s, cols_s, acc_s
):
    slot = pl.program_id(0)
    step = pl.program_id(1)
    steps = pl.num_programs(1)
    groups, _, piece, width = got_ref.shape
    per_step = TILE // piece if piece <= TILE else 1

    @pl.when(step == 0)
    def _():
        rows_s[...] = got_ref[:, 0].reshape(groups * piece, width)
        cols_s[...] = got_ref[:, 1].reshape(groups * piece, width)

    alive = first + slot < live[0]

    @pl.when(alive)
    def _():
        a = pairs[first + slot, 0]
        b = pairs[first + slot, 1]
        start = pl.multiple_of(step * TILE, TILE)
        rows = rows_s[pl.ds(start, TILE), :]
        cols = cols_s[...]
        logits = lax.dot_general(rows, cols, (((1,), (1,)), ((), ())), preferred_element_type=F32)
        row_log = jnp.log(rm_ref[pl.ds(a, 1), pl.ds(start, TILE)].astype(F32)) - LOG_TOTAL
        col_log = jnp.log(cm_ref[pl.ds(b, 1), :].astype(F32))
        row_log = jnp.transpose(jnp.broadcast_to(row_log, (8, TILE)))[:, :1]
        counts = counts_ref[0].astype(F32)
        spread = (logits + row_log + col_log) - jnp.log(jnp.maximum(counts, 1.0))
        scale = 1.0 / (counts.shape[1] ** 0.5)
        weight = 0.1 * scale + (0.25 * scale) * jnp.sqrt(counts)
        grad = jnp.where(counts > 0.0, weight * spread, scale * jax.nn.sigmoid(spread))
        delta = grad.astype(BF16)
        row_part = jnp.dot(delta, cols, preferred_element_type=F32).astype(BF16)
        for g in range(per_step):
            out_ref[step * per_step + g, 0] = row_part[g * piece : (g + 1) * piece, :]
        part = lax.dot_general(rows, delta, (((0,), (0,)), ((), ())), preferred_element_type=F32)

        @pl.when(step == 0)
        def _():
            acc_s[...] = part

        @pl.when(step > 0)
        def _():
            acc_s[...] += part

        @pl.when(step == steps - 1)
        def _():
            out_ref[:, 1] = jnp.transpose(acc_s[...]).astype(BF16).reshape(groups, piece, width)

    @pl.when(jnp.logical_not(alive) & (step == 0))
    def _():
        out_ref[...] = jnp.zeros_like(out_ref)


def items(pairs, live, got, counts, row_marginal, col_marginal, first, count):
    nodes, _, piece, width = got.shape
    blk = counts.shape[1]
    fold = piece % 16 != 0
    if fold:
        got = got.transpose(1, 0, 2, 3).reshape(1, 2 * count, nodes * piece, width)
    groups, _, rows_in, _ = got.shape
    if rows_in > TILE:
        got = got.reshape(1, 2 * count, rows_in // TILE, TILE, width)[0].transpose(1, 0, 2, 3)
        groups, rows_in = got.shape[0], TILE
    out = pl.pallas_call(
        functools.partial(item_kernel, first),
        out_shape=jax.ShapeDtypeStruct(got.shape, BF16),
        grid_spec=pltpu.PrefetchScalarGridSpec(
            num_scalar_prefetch=2,
            grid=(count, blk // TILE),
            in_specs=[
                pl.BlockSpec((groups, 2, rows_in, width), lambda s, i, *_: (0, s, 0, 0)),
                pl.BlockSpec((1, TILE, blk), lambda s, i, *_: (first + s, i, 0)),
                pl.BlockSpec(row_marginal.shape, lambda s, i, *_: (0, 0)),
                pl.BlockSpec(col_marginal.shape, lambda s, i, *_: (0, 0)),
            ],
            out_specs=pl.BlockSpec((groups, 2, rows_in, width), lambda s, i, *_: (0, s, 0, 0)),
            scratch_shapes=[
                pltpu.VMEM((blk, width), BF16),
                pltpu.VMEM((blk, width), BF16),
                pltpu.VMEM((width, blk), F32),
            ],
        ),
        compiler_params=params(),
        cost_estimate=pl.CostEstimate(
            flops=6 * count * blk * blk * width,
            bytes_accessed=count * (blk * blk * 4 + 4 * blk * width * 2),
            transcendentals=4 * count * blk * blk,
        ),
        name="items",
    )(pairs, live, got, counts, row_marginal, col_marginal)
    if fold:
        out = out.transpose(1, 0, 2, 3).reshape(2 * count, nodes, piece, width)
        out = out.transpose(1, 0, 2, 3)
    return out


def sum_kernel(first, count, req, ret_ref, row_out, col_out):
    row_out[...] = jnp.zeros_like(row_out)
    col_out[...] = jnp.zeros_like(col_out)
    add_parts(first, count, req, ret_ref, row_out, col_out)


def add_parts(first, count, req, ret_ref, row_acc, col_acc):
    def one(node, carry):
        for k in range(count):
            a = req[node, 2 * (first + k)]
            b = req[node, 2 * (first + k) + 1]
            row_acc[a] += ret_ref[node, 2 * k].astype(F32)
            col_acc[b] += ret_ref[node, 2 * k + 1].astype(F32)
        return carry

    lax.fori_loop(0, ret_ref.shape[0], one, 0)


def sums(req, ret, blocks, first, count):
    piece, width = ret.shape[2:]
    shape = jax.ShapeDtypeStruct((blocks, piece, width), F32)
    return pl.pallas_call(
        functools.partial(sum_kernel, first, count),
        out_shape=(shape, shape),
        grid_spec=pltpu.PrefetchScalarGridSpec(
            num_scalar_prefetch=1,
            in_specs=[vmem_spec()],
            out_specs=(vmem_spec(), vmem_spec()),
            grid=(),
        ),
        compiler_params=params(),
        cost_estimate=pl.CostEstimate(
            flops=ret.size,
            bytes_accessed=ret.size * 2 + 8 * blocks * piece * width,
            transcendentals=0,
        ),
        name="sums",
    )(req, ret)


def update_kernel(first, count, req, ret_ref, rg, cg, rm, ra, cm, ca, rn, ran, cn, can):
    rn[...] = rg[...]
    cn[...] = cg[...]
    add_parts(first, count, req, ret_ref, rn, cn)

    def one(block, carry):
        for master, accum, new, accum_out in ((rm, ra, rn, ran), (cm, ca, cn, can)):
            grad = new[block]
            accum_new = accum[block] + grad * grad
            accum_out[block] = accum_new
            new[block] = master[block] - LEARN_RATE * grad / jnp.sqrt(accum_new)
        return carry

    lax.fori_loop(0, rm.shape[0], one, 0)


def update(req, ret, row_grad, col_grad, row_master, row_accum, col_master, col_accum, first, count):
    shape = jax.ShapeDtypeStruct(row_master.shape, F32)
    return pl.pallas_call(
        functools.partial(update_kernel, first, count),
        out_shape=(shape,) * 4,
        grid_spec=pltpu.PrefetchScalarGridSpec(
            num_scalar_prefetch=1,
            in_specs=[vmem_spec()] * 7,
            out_specs=(vmem_spec(),) * 4,
            grid=(),
        ),
        compiler_params=params(),
        cost_estimate=pl.CostEstimate(
            flops=8 * row_master.size,
            bytes_accessed=ret.size * 2 + 40 * row_master.size,
            transcendentals=2 * row_master.size,
        ),
        name="update",
    )(req, ret, row_grad, col_grad, row_master, row_accum, col_master, col_accum)


def exchange(x):
    return lax.all_to_all(x, AXES, split_axis=0, concat_axis=0, tiled=True)


def body(
    row_master, row_accum, col_master, col_accum, pairs, live, counts, row_marginal, col_marginal
):
    slots = pairs.shape[0]
    blocks = row_master.shape[0]
    nodes = lax.axis_size(AXES)
    req = exchange(jnp.broadcast_to(pairs.reshape(1, 2 * slots), (nodes, 2 * slots)))
    cut = 1
    lists = ((0, cut), (cut, slots - cut))
    back = []
    got = [exchange(pick(req, row_master, col_master, *part)) for part in lists]
    for part, rows in zip(lists, got):
        back.append(exchange(items(pairs, live, rows, counts, row_marginal, col_marginal, *part)))
    row_grad, col_grad = sums(req, back[0], blocks, *lists[0])
    return update(
        req, back[1], row_grad, col_grad, row_master, row_accum, col_master, col_accum, *lists[1]
    )


def solution(mesh):
    table = P(None, AXES, None)
    return jax.shard_map(
        body,
        mesh=mesh,
        in_specs=(
            table,
            table,
            table,
            table,
            P(AXES, None),
            P(AXES),
            P(AXES, None, None),
            P(),
            P(),
        ),
        out_specs=(table,) * 4,
        check_vma=False,
    )
```

time: 313 us -> 195 us (0.62)
  waiting for transfers between devices: 170 us -> 121 us
  matrix products: 30.4 us -> 0 us
  Pallas kernels: 0 us -> 30.4 us
  blocking collectives: 43.5 us -> 14.3 us
  local copies, waits for them, and re-layouts: 36.8 us -> 13.4 us
  between operations: 13.2 us -> 1.44 us
  other arithmetic: 3.69 us -> 0 us
    all_to_all x4, waiting for transfers between devices: 170 us -> 121 us  [exchange(): return lax.all_to_all(x, AXES, split_axis=0, concat_axis=0, tiled=True)]
    all_gather x1 -> x0, blocking collectives: 43.5 us -> none  [body(): lax.all_gather(pairs, ('rows', 'cols'), axis=0, tiled=True)]
    dot_general x11 -> x0, matrix products: 30.4 us -> none  [the longest x3 14.3 us: slot_delta(): lax.dot_general(rows_blk, cols_blk, (((1,), (1,)), ((), ())), preferred_e...]
    pallas_call x0 -> x6, Pallas kernels: none -> 30.4 us  [the longest x2 20.3 us: items(): pl.pallas_call(functools.partial(item_kernel, first), out_shape=jax.Shape...]
    all_to_all x0 -> x1, blocking collectives: none -> 14.3 us  [exchange(): return lax.all_to_all(x, AXES, split_axis=0, concat_axis=0, tiled=True)]
    dot_general x3 -> x0, local copies, waits for them, and re-layouts: 11.8 us -> none  [block_grads(): lax.dot_general(delta, rows_blk, (((0,), (0,)), ((), ())), preferred_elem...]
    gather x4 -> x0, local copies, waits for them, and re-layouts: 6.59 us -> none  [the longest x2 4.61 us: body(): send_rows = row_master.astype(jnp.bfloat16)[row_ids]]
    unnamed x38 -> x31, local copies, waits for them, and re-layouts: 8.88 us -> 13.3 us
  transfers between devices with their start and end apart: 4 -> 4, of which waited for: 4 -> 4; matrix products, arithmetic and copies ran while one was open for 11% -> 0% of each run, Pallas kernels for 0% -> 12%
where the time goes in v1:
time: 195 us
  waiting for transfers between devices  121 us (62%)
  Pallas kernels  30.4 us (16%)
  blocking collectives  14.3 us (7%)
  starting transfers between devices  14.2 us (7%)
  local copies, waits for them, and re-layouts  13.4 us (7%)
    all_to_all x4, waiting for transfers between devices, exchange(): return lax.all_to_all(x, AXES, split_axis=0, concat_axis=0, tiled=True)  121 us
    pallas_call x2, Pallas kernels, items(): pl.pallas_call(functools.partial(item_kernel, first), out_shape=jax.Shape...  20.3 us
    all_to_all x1, blocking collectives, exchange(): return lax.all_to_all(x, AXES, split_axis=0, concat_axis=0, tiled=True)  14.3 us
    all_to_all x4, starting transfers between devices, exchange(): return lax.all_to_all(x, AXES, split_axis=0, concat_axis=0, tiled=True)  14.2 us
    unnamed x31, local copies, waits for them, and re-layouts  13.3 us
    pallas_call x1, Pallas kernels, update(): pl.pallas_call(functools.partial(update_kernel, first, count), out_shape=...  6.55 us
  transfers between devices with their start and end apart: 4, of which 4 were waited for; matrix products, arithmetic and copies ran while one was open for 0% of the time, Pallas kernels for 12%

profile of v1, /device:TPU:0, one launch (start us, length us, event | category | flops | bytes accessed | tf_op | source)
XLA Modules:
  0.0 194.7 jit_solution(6548288936152270540)
XLA Ops:
  1.5 14.3 %all_to_all.28 = s32[32,1,6]{2,1,0:T(1,128)S(1)} all-to-all(s32[32,1,6]{2,1,0:T(1,128)S(1)} %broadcast_in_dim.8), channel_id=1, replica_groups=mesh['rows'=8,'cols'=4] {'rows','cols'}, dimensions={0} | all-to-all | bytes 1536 | tf_op jit(solution)/shard_map/all_to_all | solution.py:241
  15.8 1.2 copy-done
  17.0 1.2 copy-done.2
  18.2 1.1 pick.3
  19.3 1.0 copy-done.7
  20.3 2.6 %all-to-all-start.3 = ((bf16[32,2,32,256]{3,2,1,0:T(8,128)(2,1)}), bf16[32,2,32,256]{3,2,1,0:T(8,128)(2,1)S(1)}, u32[]{:S(2)}, u32[]{:S(2)}) async-start(bf16[32,2,32,256]{3,2,1,0:T(8,128)(2,1)} %copy-done.7), calls=%async_computation.3 | async-start | bytes 2097152 | tf_op jit(solution)/shard_map/all_to_all | solution.py:241
  23.0 1.2 pick.2
  24.2 1.3 copy-done.4
  25.5 23.7 %all-to-all-done.3.got_ref = bf16[32,2,32,256]{3,2,1,0:T(8,128)(2,1)S(1)} async-done(((bf16[32,2,32,256]{3,2,1,0:T(8,128)(2,1)}), bf16[32,2,32,256]{3,2,1,0:T(8,128)(2,1)S(1)}, u32[]{:S(2)}, u32[]{:S(2)}) %all-to-all-start.3) | async-done | bytes 1048608 | tf_op jit(solution)/shard_map/all_to_all | solution.py:241
  49.2 3.7 %all-to-all-start.1 = ((bf16[32,4,32,256]{3,2,1,0:T(8,128)(2,1)}), bf16[32,4,32,256]{3,2,1,0:T(8,128)(2,1)}, u32[]{:S(2)}, u32[]{:S(2)}) async-start(bf16[32,4,32,256]{3,2,1,0:T(8,128)(2,1)} %copy-done.4), calls=%async_computation.1 | async-start | bytes 4194304 | tf_op jit(solution)/shard_map/all_to_all | solution.py:241
  53.5 7.1 %items.3 = bf16[32,2,32,256]{3,2,1,0:T(8,128)(2,1)S(1)} custom-call(s32[3,2]{1,0:T(4,128)S(1)} %copy.19.pairs, s32[1]{0:T(128)S(6)} %copy.22.live, bf16[32,2,32,256]{3,2,1,0:T(8,128)(2,1)S(1)} %all-to-all-done.3.got_ref, s32[3,1024,1024]{2,1,0:T(8,128)} %counts_ref.3, s32[32,1024]{1,0:T(8,128)S(1)} %copy-done.13, s32[32,1024]{1,0:T(8,128)S(1)} %copy-done.14), custom_call_target="tpu_custom_call" | custom-call | flops 1610612736 | bytes 6291456 | tf_op jit(solution)/shard_map/items/pallas_call | solution.py:130
  61.6 40.0 %all-to-all-done.1.got_ref = bf16[32,4,32,256]{3,2,1,0:T(8,128)(2,1)} async-done(((bf16[32,4,32,256]{3,2,1,0:T(8,128)(2,1)}), bf16[32,4,32,256]{3,2,1,0:T(8,128)(2,1)}, u32[]{:S(2)}, u32[]{:S(2)}) %all-to-all-start.1) | async-done | bytes 2097184 | tf_op jit(solution)/shard_map/all_to_all | solution.py:241
  101.6 4.1 %all-to-all-start.4 = ((bf16[32,2,32,256]{3,2,1,0:T(8,128)(2,1)}), bf16[32,2,32,256]{3,2,1,0:T(8,128)(2,1)S(1)}, u32[]{:S(2)}, u32[]{:S(2)}) async-start(bf16[32,2,32,256]{3,2,1,0:T(8,128)(2,1)} %copy-done.6), calls=%async_computation.4 | async-start | bytes 2097152 | tf_op jit(solution)/shard_map/all_to_all | solution.py:241
  105.7 13.1 %items.2 = bf16[32,4,32,256]{3,2,1,0:T(8,128)(2,1)S(1)} custom-call(s32[3,2]{1,0:T(4,128)S(1)} %copy.19.pairs, s32[1]{0:T(128)S(6)} %copy.22.live, bf16[32,4,32,256]{3,2,1,0:T(8,128)(2,1)} %all-to-all-done.1.got_ref, s32[3,1024,1024]{2,1,0:T(8,128)} %counts_ref.3, s32[32,1024]{1,0:T(8,128)S(1)} %copy-done.13, s32[32,1024]{1,0:T(8,128)S(1)} %copy-done.14), custom_call_target="tpu_custom_call" | custom-call | flops 3221225472 | bytes 12582912 | tf_op jit(solution)/shard_map/items/pallas_call | solution.py:130
  118.9 1.3 copy-done.5
  120.1 11.8 %all-to-all-done.4.ret_ref = bf16[32,2,32,256]{3,2,1,0:T(8,128)(2,1)S(1)} async-done(((bf16[32,2,32,256]{3,2,1,0:T(8,128)(2,1)}), bf16[32,2,32,256]{3,2,1,0:T(8,128)(2,1)S(1)}, u32[]{:S(2)}, u32[]{:S(2)}) %all-to-all-start.4) | async-done | bytes 1048608 | tf_op jit(solution)/shard_map/all_to_all | solution.py:241
  131.9 3.7 %all-to-all-start.2 = ((bf16[32,4,32,256]{3,2,1,0:T(8,128)(2,1)}), bf16[32,4,32,256]{3,2,1,0:T(8,128)(2,1)}, u32[]{:S(2)}, u32[]{:S(2)}) async-start(bf16[32,4,32,256]{3,2,1,0:T(8,128)(2,1)} %copy-done.5), calls=%async_computation.2 | async-start | bytes 4194304 | tf_op jit(solution)/shard_map/all_to_all | solution.py:241
  135.7 1.3 sums.1
  137.9 1.0 copy-done.11
  138.9 45.5 %all-to-all-done.2.ret_ref = bf16[32,4,32,256]{3,2,1,0:T(8,128)(2,1)} async-done(((bf16[32,4,32,256]{3,2,1,0:T(8,128)(2,1)}), bf16[32,4,32,256]{3,2,1,0:T(8,128)(2,1)}, u32[]{:S(2)}, u32[]{:S(2)}) %all-to-all-start.2) | async-done | bytes 2097184 | tf_op jit(solution)/shard_map/all_to_all | solution.py:241
  184.4 1.2 copy-done.8
  185.7 1.2 copy-done.10
  186.9 1.2 copy-done.12
  188.1 6.5 %update.1 = (f32[32,32,256]{2,1,0:T(8,128)}, f32[32,32,256]{2,1,0:T(8,128)}, f32[32,32,256]{2,1,0:T(8,128)}, f32[32,32,256]{2,1,0:T(8,128)}) custom-call(s32[32,6]{1,0:T(8,128)S(1)} %bitcast.4, bf16[32,4,32,256]{3,2,1,0:T(8,128)(2,1)} %all-to-all-done.2.ret_ref, f32[32,32,256]{2,1,0:T(8,128)S(1)} %copy-done.10, f32[32,32,256]{2,1,0:T(8,128)S(1)} %copy-done.12, ...), custom_call_target="tpu_custom_call" | custom-call | flops 2097152 | bytes 12582912 | tf_op jit(solution)/shard_map/update/pallas_call | solution.py:221
  (24 shorter events, 2.8 us)
Async XLA Ops:
  15.8 1.2 copy-start
  17.0 1.2 copy-start.2
  18.2 4.7 %copy-start.1 = (f32[32,32,256]{2,1,0:T(8,128)S(1)}, f32[32,32,256]{2,1,0:T(8,128)}, u32[]{:S(2)}) copy-start(f32[32,32,256]{2,1,0:T(8,128)} %rm.1) | copy-start | bytes 3145732
  18.2 4.8 %copy-start.3 = (f32[32,32,256]{2,1,0:T(8,128)S(1)}, f32[32,32,256]{2,1,0:T(8,128)}, u32[]{:S(2)}) copy-start(f32[32,32,256]{2,1,0:T(8,128)} %cm.1) | copy-start | bytes 3145732
  19.3 1.0 copy-start.7
  20.3 28.9 %all-to-all-start.3 = ((bf16[32,2,32,256]{3,2,1,0:T(8,128)(2,1)}), bf16[32,2,32,256]{3,2,1,0:T(8,128)(2,1)S(1)}, u32[]{:S(2)}, u32[]{:S(2)}) async-start(bf16[32,2,32,256]{3,2,1,0:T(8,128)(2,1)} %copy-done.7), calls=%async_computation.3 | async-start | bytes 2097152 | tf_op jit(solution)/shard_map/all_to_all | solution.py:241
  24.2 1.3 copy-start.4
  25.5 28.0 %copy-start.13 = (s32[32,1024]{1,0:T(8,128)S(1)}, s32[32,1024]{1,0:T(8,128)}, u32[]{:S(2)}) copy-start(s32[32,1024]{1,0:T(8,128)} %rm_ref.3) | copy-start | bytes 393220
  25.5 28.0 %copy-start.14 = (s32[32,1024]{1,0:T(8,128)S(1)}, s32[32,1024]{1,0:T(8,128)}, u32[]{:S(2)}) copy-start(s32[32,1024]{1,0:T(8,128)} %cm_ref.3) | copy-start | bytes 393220
  49.2 52.4 %all-to-all-start.1 = ((bf16[32,4,32,256]{3,2,1,0:T(8,128)(2,1)}), bf16[32,4,32,256]{3,2,1,0:T(8,128)(2,1)}, u32[]{:S(2)}, u32[]{:S(2)}) async-start(bf16[32,4,32,256]{3,2,1,0:T(8,128)(2,1)} %copy-done.4), calls=%async_computation.1 | async-start | bytes 4194304 | tf_op jit(solution)/shard_map/all_to_all | solution.py:241
  60.6 1.0 copy-start.6
  101.6 30.3 %all-to-all-start.4 = ((bf16[32,2,32,256]{3,2,1,0:T(8,128)(2,1)}), bf16[32,2,32,256]{3,2,1,0:T(8,128)(2,1)S(1)}, u32[]{:S(2)}, u32[]{:S(2)}) async-start(bf16[32,2,32,256]{3,2,1,0:T(8,128)(2,1)} %copy-done.6), calls=%async_computation.4 | async-start | bytes 2097152 | tf_op jit(solution)/shard_map/all_to_all | solution.py:241
  118.8 1.3 copy-start.5
  131.9 52.5 %all-to-all-start.2 = ((bf16[32,4,32,256]{3,2,1,0:T(8,128)(2,1)}), bf16[32,4,32,256]{3,2,1,0:T(8,128)(2,1)}, u32[]{:S(2)}, u32[]{:S(2)}) async-start(bf16[32,4,32,256]{3,2,1,0:T(8,128)(2,1)} %copy-done.5), calls=%async_computation.2 | async-start | bytes 4194304 | tf_op jit(solution)/shard_map/all_to_all | solution.py:241
  137.0 1.0 copy-start.9
  137.9 1.0 copy-start.11
  184.4 1.2 copy-start.8
  185.7 1.2 copy-start.10
  186.9 1.2 copy-start.12

commit v2 on v1

v2 whole, which is shorter than its diff:
```python
import functools

import jax
import jax.numpy as jnp
from jax import lax
from jax.experimental import pallas as pl
from jax.experimental.pallas import tpu as pltpu
from jax.sharding import PartitionSpec as P

LOG_TOTAL = 14.3
LEARN_RATE = 0.05
AXES = ("rows", "cols")
TILE = 256
VMEM_LIMIT = 60 * 1024 * 1024

BF16 = jnp.bfloat16
F32 = jnp.float32


def vmem_spec():
    return pl.BlockSpec(memory_space=pltpu.VMEM)


def params():
    return pltpu.CompilerParams(vmem_limit_bytes=VMEM_LIMIT)


def pick_kernel(req, row_ref, col_ref, out_ref, held, sems):
    nodes, lists = out_ref.shape[:2]
    chunks = sems.shape[0]
    span = nodes // chunks
    copies = []
    for chunk in range(chunks):

        def one(i, carry, base=chunk * span):
            node = base + i
            for k in range(0, lists, 2):
                held[node, k] = row_ref[req[node, k]]
                held[node, k + 1] = col_ref[req[node, k + 1]]
            return carry

        lax.fori_loop(0, span, one, 0)
        part = pl.ds(chunk * span, span)
        copy = pltpu.make_async_copy(held.at[part], out_ref.at[part], sems.at[chunk])
        copy.start()
        copies.append(copy)
    for copy in copies:
        copy.wait()


def pick(req, rows, cols):
    nodes, lists = req.shape
    piece, width = rows.shape[1:]
    return pl.pallas_call(
        pick_kernel,
        out_shape=jax.ShapeDtypeStruct((nodes, lists, piece, width), BF16),
        grid_spec=pltpu.PrefetchScalarGridSpec(
            num_scalar_prefetch=1,
            grid=(),
            in_specs=[vmem_spec()] * 2,
            out_specs=pl.BlockSpec(memory_space=pltpu.HBM),
            scratch_shapes=[
                pltpu.VMEM((nodes, lists, piece, width), BF16),
                pltpu.SemaphoreType.DMA((8,)),
            ],
        ),
        compiler_params=pltpu.CompilerParams(vmem_limit_bytes=16 * 1024 * 1024),
        cost_estimate=pl.CostEstimate(
            flops=0,
            bytes_accessed=4 * rows.size + nodes * lists * piece * width * 2,
            transcendentals=0,
        ),
        name="pick",
    )(req, rows, cols)


def item_kernel(first, pairs, live, rows_ref, cols_ref, *refs):
    *count_refs, rm_ref, cm_ref, out_ref = refs
    slot = first + pl.program_id(0)
    groups, _, piece, width = rows_ref.shape
    blk = groups * piece
    alive = slot < live[0]

    @pl.when(alive)
    def _():
        a = pairs[slot, 0]
        b = pairs[slot, 1]
        cols = cols_ref[...].reshape(blk, width)
        col_log = jnp.log(cm_ref[pl.ds(b, 1), :].astype(F32))
        scale = 1.0 / (blk**0.5)
        parts = []
        deltas = []
        for start, counts_ref in zip(range(0, blk, TILE), count_refs):
            span = slice(start // piece, (start + TILE) // piece)
            rows = rows_ref[span].reshape(TILE, width)
            logits = lax.dot_general(
                rows, cols, (((1,), (1,)), ((), ())), preferred_element_type=F32
            )
            row_log = jnp.log(rm_ref[pl.ds(a, 1), start : start + TILE].astype(F32)) - LOG_TOTAL
            row_log = jnp.transpose(jnp.broadcast_to(row_log, (8, TILE)))[:, :1]
            counts = counts_ref[0].astype(F32)
            seen = jnp.maximum(counts, 1.0)
            spread = ((logits + row_log) + col_log) - jnp.log(seen)
            weight = 0.1 * scale + (0.25 * scale) * (seen * lax.rsqrt(seen))
            unseen = (0.5 * scale) * jnp.tanh(0.5 * spread) + 0.5 * scale
            delta = jnp.where(counts > 0.0, weight * spread, unseen).astype(BF16)
            row_part = jnp.dot(delta, cols, preferred_element_type=F32).astype(BF16)
            out_ref[span, 0] = row_part.reshape(TILE // piece, piece, width)
            parts.append(rows)
            deltas.append(delta)
        col_part = lax.dot_general(
            jnp.concatenate(parts, 0),
            jnp.concatenate(deltas, 0),
            (((0,), (0,)), ((), ())),
            preferred_element_type=F32,
        )
        out_ref[:, 1] = jnp.transpose(col_part).astype(BF16).reshape(groups, piece, width)

    @pl.when(jnp.logical_not(alive))
    def _():
        out_ref[...] = jnp.zeros_like(out_ref)


def join(got):
    nodes, lists, piece, width = got.shape
    if piece % 16 == 0:
        return got
    got = got.transpose(1, 0, 2, 3).reshape(lists, nodes * piece // TILE, TILE, width)
    return got.transpose(1, 0, 2, 3)


def cut(out, nodes, piece):
    groups, lists, rows, width = out.shape
    if rows == piece:
        return out
    out = out.transpose(1, 0, 2, 3).reshape(lists, nodes, piece, width)
    return out.transpose(1, 0, 2, 3)


def items(pairs, live, got, counts, row_marginal, col_marginal, first, count):
    nodes, _, piece, width = got.shape
    blk = counts.shape[1]
    got = join(got)
    groups, lists, rows_in, _ = got.shape
    whole = pl.BlockSpec(row_marginal.shape, lambda s, *_: (0, 0))
    tiles = blk // TILE

    def table(k):
        return pl.BlockSpec((groups, 1, rows_in, width), lambda s, *_: (0, 2 * (first + s) + k, 0, 0))

    def chunk(i):
        return pl.BlockSpec((1, TILE, blk), lambda s, *_: (first + s, i, 0))

    out = pl.pallas_call(
        functools.partial(item_kernel, first),
        out_shape=jax.ShapeDtypeStruct((groups, 2 * count, rows_in, width), BF16),
        grid_spec=pltpu.PrefetchScalarGridSpec(
            num_scalar_prefetch=2,
            grid=(count,),
            in_specs=[
                table(0),
                table(1),
                *(chunk(i) for i in range(tiles)),
                whole,
                whole,
            ],
            out_specs=pl.BlockSpec((groups, 2, rows_in, width), lambda s, *_: (0, s, 0, 0)),
        ),
        compiler_params=params(),
        cost_estimate=pl.CostEstimate(
            flops=6 * count * blk * blk * width,
            bytes_accessed=count * (blk * blk * 4 + 4 * blk * width * 2),
            transcendentals=3 * count * blk * blk,
        ),
        name="items",
    )(pairs, live, got, got, *([counts] * tiles), row_marginal, col_marginal)
    return cut(out, nodes, piece)


def add_parts(first, req, ret_ref, row_acc, col_acc):
    def one(node, carry):
        for k in range(0, ret_ref.shape[1], 2):
            row_acc[req[node, first + k]] += ret_ref[node, k].astype(F32)
            col_acc[req[node, first + k + 1]] += ret_ref[node, k + 1].astype(F32)
        return carry

    lax.fori_loop(0, ret_ref.shape[0], one, 0)


def sum_kernel(req, ret_ref, row_out, col_out):
    row_out[...] = jnp.zeros_like(row_out)
    col_out[...] = jnp.zeros_like(col_out)
    add_parts(0, req, ret_ref, row_out, col_out)


def sums(req, ret, blocks):
    piece, width = ret.shape[2:]
    shape = jax.ShapeDtypeStruct((blocks, piece, width), F32)
    return pl.pallas_call(
        sum_kernel,
        out_shape=(shape, shape),
        grid_spec=pltpu.PrefetchScalarGridSpec(
            num_scalar_prefetch=1,
            in_specs=[vmem_spec()],
            out_specs=(vmem_spec(), vmem_spec()),
            grid=(),
        ),
        compiler_params=params(),
        cost_estimate=pl.CostEstimate(
            flops=ret.size,
            bytes_accessed=ret.size * 2 + 8 * blocks * piece * width,
            transcendentals=0,
        ),
        name="sums",
    )(req, ret)


def update_kernel(first, req, ret_ref, rg, cg, rm, ra, cm, ca, rn, ran, cn, can, row_s, col_s):
    row_s[...] = rg[...]
    col_s[...] = cg[...]
    add_parts(first, req, ret_ref, row_s, col_s)
    for grads, master, accum, new, accum_out in ((row_s, rm, ra, rn, ran), (col_s, cm, ca, cn, can)):
        grad = grads[...]
        accum_new = accum[...] + grad * grad
        accum_out[...] = accum_new
        new[...] = master[...] - LEARN_RATE * grad * lax.rsqrt(accum_new)


def update(req, ret, row_grad, col_grad, row_master, row_accum, col_master, col_accum, first):
    blocks, piece, width = row_master.shape
    nodes, lists = ret.shape[:2]
    shape = jax.ShapeDtypeStruct(row_master.shape, F32)
    rows = piece if piece % 16 else 16
    table = pl.BlockSpec((blocks, rows, width), lambda i, *_: (0, i, 0))
    return pl.pallas_call(
        functools.partial(update_kernel, first),
        out_shape=(shape,) * 4,
        grid_spec=pltpu.PrefetchScalarGridSpec(
            num_scalar_prefetch=1,
            grid=(piece // rows,),
            in_specs=[pl.BlockSpec((nodes, lists, rows, width), lambda i, *_: (0, 0, i, 0))]
            + [table] * 6,
            out_specs=(table,) * 4,
            scratch_shapes=[pltpu.VMEM((blocks, rows, width), F32)] * 2,
        ),
        compiler_params=params(),
        cost_estimate=pl.CostEstimate(
            flops=8 * row_master.size,
            bytes_accessed=ret.size * 2 + 40 * row_master.size,
            transcendentals=2 * row_master.size,
        ),
        name="update",
    )(req, ret, row_grad, col_grad, row_master, row_accum, col_master, col_accum)


def exchange(x):
    return lax.all_to_all(x, AXES, split_axis=0, concat_axis=0, tiled=True)


def body(
    row_master, row_accum, col_master, col_accum, pairs, live, counts, row_marginal, col_marginal
):
    slots = pairs.shape[0]
    blocks = row_master.shape[0]
    nodes = lax.axis_size(AXES)
    req = exchange(jnp.broadcast_to(pairs.reshape(1, 2 * slots), (nodes, 2 * slots)))
    got = exchange(pick(req, row_master.astype(BF16), col_master.astype(BF16)))
    lead = 1
    back = items(pairs, live, got, counts, row_marginal, col_marginal, 0, lead)
    back = exchange(back)
    rest = items(pairs, live, got, counts, row_marginal, col_marginal, lead, slots - lead)
    rest, back = lax.optimization_barrier((rest, back))
    rest = exchange(rest)
    row_grad, col_grad = sums(req, back, blocks)
    return update(
        req, rest, row_grad, col_grad, row_master, row_accum, col_master, col_accum, 2 * lead
    )


def solution(mesh):
    table = P(None, AXES, None)
    return jax.shard_map(
        body,
        mesh=mesh,
        in_specs=(
            table,
            table,
            table,
            table,
            P(AXES, None),
            P(AXES),
            P(AXES, None, None),
            P(),
            P(),
        ),
        out_specs=(table,) * 4,
        check_vma=False,
    )
```

time: 195 us -> 194 us (level)
  blocking collectives: 14.3 us -> 0 us
  waiting for transfers between devices: 121 us -> 135 us
  local copies, waits for them, and re-layouts: 13.4 us -> 2.81 us
  starting transfers between devices: 14.2 us -> 18.8 us
  other arithmetic: 0 us -> 2.59 us
  Pallas kernels: 30.4 us -> 32.8 us
    all_to_all x1 -> x0, blocking collectives: 14.3 us -> none  [exchange(): return lax.all_to_all(x, AXES, split_axis=0, concat_axis=0, tiled=True)]
    all_to_all x4, waiting for transfers between devices: 121 us -> 135 us  [exchange(): return lax.all_to_all(x, AXES, split_axis=0, concat_axis=0, tiled=True)]
    unnamed x31 -> x9, local copies, waits for them, and re-layouts: 13.3 us -> 2.11 us
    all_to_all x4, starting transfers between devices: 14.2 us -> 18.8 us  [exchange(): return lax.all_to_all(x, AXES, split_axis=0, concat_axis=0, tiled=True)]
    pallas_call x4 -> x3, Pallas kernels: 10.2 us -> 13 us  [the longest x1 6.44 us: update(): pl.pallas_call(functools.partial(update_kernel, first), out_shape=(shape,...]
    convert_element_type x0 -> x2, other arithmetic: none -> 2.59 us  [body(): got = exchange(pick(req, row_master.astype(BF16), col_master.astype(BF16)))]
  transfers between devices with their start and end apart: 4 -> 4, of which waited for: 4 -> 4; matrix products, arithmetic and copies ran while one was open for 0% -> 1% of each run, Pallas kernels for 12% -> 8%
where the time goes in v2:
time: 194 us; the launch traced here: 193 us
  waiting for transfers between devices  135 us (70%)
  Pallas kernels  32.8 us (17%)
  starting transfers between devices  18.8 us (10%)
  local copies, waits for them, and re-layouts  2.81 us (1%)
  other arithmetic  2.59 us (1%)
    all_to_all x4, waiting for transfers between devices, exchange(): return lax.all_to_all(x, AXES, split_axis=0, concat_axis=0, tiled=True)  135 us
    pallas_call x2, Pallas kernels, items(): pl.pallas_call(functools.partial(item_kernel, first), out_shape=jax.Shape...  19.8 us
    all_to_all x4, starting transfers between devices, exchange(): return lax.all_to_all(x, AXES, split_axis=0, concat_axis=0, tiled=True)  18.8 us
    pallas_call x1, Pallas kernels, update(): pl.pallas_call(functools.partial(update_kernel, first), out_shape=(shape,...  6.44 us
    pallas_call x1, Pallas kernels, sums(): pl.pallas_call(sum_kernel, out_shape=(shape, shape), grid_spec=pltpu.Pref...  3.99 us
  transfers between devices with their start and end apart: 4, of which 4 were waited for; matrix products, arithmetic and copies ran while one was open for 1% of the time, Pallas kernels for 8%

profile of v2, /device:TPU:0, one launch (start us, length us, event | category | flops | bytes accessed | tf_op | source)
XLA Modules:
  0.0 193.1 jit_solution(1687768557631137038)
XLA Ops:
  0.6 0.8 copy.19.pairs
  1.4 0.0 copy-start.3
  1.4 0.1 broadcast_in_dim.7
  1.5 0.6 broadcast_in_dim.8
  2.1 7.3 %all-to-all-start = ((s32[32,1,6]{2,1,0:T(1,128)}), s32[32,1,6]{2,1,0:T(1,128)S(1)}, u32[]{:S(2)}, u32[]{:S(2)}) async-start(s32[32,1,6]{2,1,0:T(1,128)} %broadcast_in_dim.8), calls=%async_computation | async-start | bytes 32768 | tf_op jit(solution)/shard_map/all_to_all | solution.py:257
  9.4 1.3 convert_element_type.6.row_ref
  10.7 1.3 convert_element_type.7.col_ref
  12.0 4.5 %all-to-all-done = s32[32,1,6]{2,1,0:T(1,128)S(1)} async-done(((s32[32,1,6]{2,1,0:T(1,128)}), s32[32,1,6]{2,1,0:T(1,128)S(1)}, u32[]{:S(2)}, u32[]{:S(2)}) %all-to-all-start) | async-done | bytes 800 | tf_op jit(solution)/shard_map/all_to_all | solution.py:257
  16.5 0.0 copy-start
  16.5 2.6 %pick.1 = bf16[32,6,32,256]{3,2,1,0:T(8,128)(2,1)} custom-call(s32[32,6]{1,0:T(8,128)S(1)} %bitcast.1, bf16[32,32,256]{2,1,0:T(8,128)(2,1)S(1)} %convert_element_type.6.row_ref, bf16[32,32,256]{2,1,0:T(8,128)(2,1)S(1)} %convert_element_type.7.col_ref), custom_call_target="tpu_custom_call" | custom-call | bytes 4194304 | tf_op jit(solution)/shard_map/pick/pallas_call | solution.py:54
  19.1 0.0 copy-done.3
  19.1 0.0 copy-done
  19.1 3.5 %all-to-all-start.1 = ((bf16[32,6,32,256]{3,2,1,0:T(8,128)(2,1)}), bf16[32,6,32,256]{3,2,1,0:T(8,128)(2,1)}, u32[]{:S(2)}, u32[]{:S(2)}) async-start(bf16[32,6,32,256]{3,2,1,0:T(8,128)(2,1)} %pick.1), calls=%async_computation.1 | async-start | bytes 6291456 | tf_op jit(solution)/shard_map/all_to_all | solution.py:257
  23.3 71.1 %all-to-all-done.1.rows_ref.cols_ref = bf16[32,6,32,256]{3,2,1,0:T(8,128)(2,1)} async-done(((bf16[32,6,32,256]{3,2,1,0:T(8,128)(2,1)}), bf16[32,6,32,256]{3,2,1,0:T(8,128)(2,1)}, u32[]{:S(2)}, u32[]{:S(2)}) %all-to-all-start.1) | async-done | bytes 3145760 | tf_op jit(solution)/shard_map/all_to_all | solution.py:257
  94.5 7.9 %items.3 = bf16[32,2,32,256]{3,2,1,0:T(8,128)(2,1)} custom-call(s32[3,2]{1,0:T(4,128)} %copy-done.3, s32[1]{0:T(128)S(6)} %copy.22.live, bf16[32,6,32,256]{3,2,1,0:T(8,128)(2,1)} %all-to-all-done.1.rows_ref.cols_ref, bf16[32,6,32,256]{3,2,1,0:T(8,128)(2,1)} %all-to-all-done.1.rows_ref.cols_ref, s32[3,1024,1024]{2,1,0:T(8,128)} %refs_3_.3, ...), custom_call_target="tpu_custom_call" | custom-call | flops 1610612736 | bytes 6291456 | tf_op jit(solution)/shard_map/items/pallas_call | solution.py:154
  102.3 4.4 %all-to-all-start.2 = ((bf16[32,2,32,256]{3,2,1,0:T(8,128)(2,1)}), bf16[32,2,32,256]{3,2,1,0:T(8,128)(2,1)S(1)}, u32[]{:S(2)}, u32[]{:S(2)}) async-start(bf16[32,2,32,256]{3,2,1,0:T(8,128)(2,1)} %items.3), calls=%async_computation.2 | async-start | bytes 2097152 | tf_op jit(solution)/shard_map/all_to_all | solution.py:257
  106.7 11.9 %items.2 = bf16[32,4,32,256]{3,2,1,0:T(8,128)(2,1)} custom-call(s32[3,2]{1,0:T(4,128)} %copy-done.3, s32[1]{0:T(128)S(6)} %copy.22.live, bf16[32,6,32,256]{3,2,1,0:T(8,128)(2,1)} %all-to-all-done.1.rows_ref.cols_ref, bf16[32,6,32,256]{3,2,1,0:T(8,128)(2,1)} %all-to-all-done.1.rows_ref.cols_ref, s32[3,1024,1024]{2,1,0:T(8,128)} %refs_3_.3, ...), custom_call_target="tpu_custom_call" | custom-call | flops 3221225472 | bytes 12582912 | tf_op jit(solution)/shard_map/items/pallas_call | solution.py:154
  118.6 14.3 %all-to-all-done.2.ret_ref = bf16[32,2,32,256]{3,2,1,0:T(8,128)(2,1)S(1)} async-done(((bf16[32,2,32,256]{3,2,1,0:T(8,128)(2,1)}), bf16[32,2,32,256]{3,2,1,0:T(8,128)(2,1)S(1)}, u32[]{:S(2)}, u32[]{:S(2)}) %all-to-all-start.2) | async-done | bytes 1048608 | tf_op jit(solution)/shard_map/all_to_all | solution.py:257
  133.0 3.6 %all-to-all-start.3 = ((bf16[32,4,32,256]{3,2,1,0:T(8,128)(2,1)}), bf16[32,4,32,256]{3,2,1,0:T(8,128)(2,1)S(1)}, u32[]{:S(2)}, u32[]{:S(2)}) async-start(bf16[32,4,32,256]{3,2,1,0:T(8,128)(2,1)} %items.2), calls=%async_computation.3 | async-start | bytes 4194304 | tf_op jit(solution)/shard_map/all_to_all | solution.py:257
  136.6 0.0 copy-done.2
  136.6 4.0 %sums.1 = (f32[32,32,256]{2,1,0:T(8,128)}, f32[32,32,256]{2,1,0:T(8,128)}) custom-call(s32[32,6]{1,0:T(8,128)} %bitcast.2, bf16[32,2,32,256]{3,2,1,0:T(8,128)(2,1)} %copy-done.2), custom_call_target="tpu_custom_call" | custom-call | flops 524288 | bytes 3145728 | tf_op jit(solution)/shard_map/sums/pallas_call | solution.py:199
  140.6 44.8 %all-to-all-done.3.ret_ref = bf16[32,4,32,256]{3,2,1,0:T(8,128)(2,1)S(1)} async-done(((bf16[32,4,32,256]{3,2,1,0:T(8,128)(2,1)}), bf16[32,4,32,256]{3,2,1,0:T(8,128)(2,1)S(1)}, u32[]{:S(2)}, u32[]{:S(2)}) %all-to-all-start.3) | async-done | bytes 2097184 | tf_op jit(solution)/shard_map/all_to_all | solution.py:257
  185.4 1.3 copy-done.1
  186.7 6.4 %update.1 = (f32[32,32,256]{2,1,0:T(8,128)}, f32[32,32,256]{2,1,0:T(8,128)}, f32[32,32,256]{2,1,0:T(8,128)}, f32[32,32,256]{2,1,0:T(8,128)}) custom-call(s32[32,6]{1,0:T(8,128)} %bitcast.3, bf16[32,4,32,256]{3,2,1,0:T(8,128)(2,1)} %copy-done.1, f32[32,32,256]{2,1,0:T(8,128)} %get-tuple-element.10.rg, f32[32,32,256]{2,1,0:T(8,128)} %get-tuple-element.11.cg, ...), custom_call_target="tpu_custom_call" | custom-call | flops 2097152 | bytes 12582912 | tf_op jit(solution)/shard_map/update/pallas_call | solution.py:235
  (2 shorter events, 0.0 us)
Async XLA Ops:
  1.4 17.7 %copy-start.3 = (s32[3,2]{1,0:T(4,128)}, s32[3,2]{1,0:T(4,128)S(1)}, u32[]{:S(2)}) copy-start(s32[3,2]{1,0:T(4,128)S(1)} %copy.19.pairs) | copy-start | bytes 76
  2.1 14.4 %all-to-all-start = ((s32[32,1,6]{2,1,0:T(1,128)}), s32[32,1,6]{2,1,0:T(1,128)S(1)}, u32[]{:S(2)}, u32[]{:S(2)}) async-start(s32[32,1,6]{2,1,0:T(1,128)} %broadcast_in_dim.8), calls=%async_computation | async-start | bytes 32768 | tf_op jit(solution)/shard_map/all_to_all | solution.py:257
  16.5 2.6 %copy-start = (s32[32,1,6]{2,1,0:T(1,128)}, s32[32,1,6]{2,1,0:T(1,128)S(1)}, u32[]{:S(2)}) copy-start(s32[32,1,6]{2,1,0:T(1,128)S(1)} %all-to-all-done) | copy-start | bytes 2308
  19.1 75.3 %all-to-all-start.1 = ((bf16[32,6,32,256]{3,2,1,0:T(8,128)(2,1)}), bf16[32,6,32,256]{3,2,1,0:T(8,128)(2,1)}, u32[]{:S(2)}, u32[]{:S(2)}) async-start(bf16[32,6,32,256]{3,2,1,0:T(8,128)(2,1)} %pick.1), calls=%async_computation.1 | async-start | bytes 6291456 | tf_op jit(solution)/shard_map/all_to_all | solution.py:257
  102.3 30.6 %all-to-all-start.2 = ((bf16[32,2,32,256]{3,2,1,0:T(8,128)(2,1)}), bf16[32,2,32,256]{3,2,1,0:T(8,128)(2,1)S(1)}, u32[]{:S(2)}, u32[]{:S(2)}) async-start(bf16[32,2,32,256]{3,2,1,0:T(8,128)(2,1)} %items.3), calls=%async_computation.2 | async-start | bytes 2097152 | tf_op jit(solution)/shard_map/all_to_all | solution.py:257
  133.0 3.6 %copy-start.2 = (bf16[32,2,32,256]{3,2,1,0:T(8,128)(2,1)}, bf16[32,2,32,256]{3,2,1,0:T(8,128)(2,1)S(1)}, u32[]{:S(2)}) copy-start(bf16[32,2,32,256]{3,2,1,0:T(8,128)(2,1)S(1)} %all-to-all-done.2.ret_ref) | copy-start | bytes 3145732
  133.0 52.4 %all-to-all-start.3 = ((bf16[32,4,32,256]{3,2,1,0:T(8,128)(2,1)}), bf16[32,4,32,256]{3,2,1,0:T(8,128)(2,1)S(1)}, u32[]{:S(2)}, u32[]{:S(2)}) async-start(bf16[32,4,32,256]{3,2,1,0:T(8,128)(2,1)} %items.2), calls=%async_computation.3 | async-start | bytes 4194304 | tf_op jit(solution)/shard_map/all_to_all | solution.py:257
  185.4 1.3 copy-start.1

commit v3 on v2

--- a/solution.py
+++ b/solution.py
@@ -11,7 +11,8 @@
 LEARN_RATE = 0.05
 AXES = ("rows", "cols")
 TILE = 256
-VMEM_LIMIT = 60 * 1024 * 1024
+VMEM_LIMIT = 65280 * 1024
+TILE = 256
 
 BF16 = jnp.bfloat16
 F32 = jnp.float32
@@ -21,11 +22,15 @@
     return pl.BlockSpec(memory_space=pltpu.VMEM)
 
 
+def hbm_spec():
+    return pl.BlockSpec(memory_space=pltpu.HBM)
+
+
 def params():
     return pltpu.CompilerParams(vmem_limit_bytes=VMEM_LIMIT)
 
 
-def pick_kernel(req, row_ref, col_ref, out_ref, held, sems):
+def pick_kernel(first, req, row_ref, col_ref, out_ref, held, sems):
     nodes, lists = out_ref.shape[:2]
     chunks = sems.shape[0]
     span = nodes // chunks
@@ -35,8 +40,8 @@
         def one(i, carry, base=chunk * span):
             node = base + i
             for k in range(0, lists, 2):
-                held[node, k] = row_ref[req[node, k]]
-                held[node, k + 1] = col_ref[req[node, k + 1]]
+                held[node, k] = row_ref[req[node, 2 * first + k]]
+                held[node, k + 1] = col_ref[req[node, 2 * first + k + 1]]
             return carry
 
         lax.fori_loop(0, span, one, 0)
@@ -48,17 +53,18 @@
         copy.wait()
 
 
-def pick(req, rows, cols):
-    nodes, lists = req.shape
+def pick(req, rows, cols, first, count):
+    nodes = req.shape[0]
+    lists = 2 * count
     piece, width = rows.shape[1:]
     return pl.pallas_call(
-        pick_kernel,
+        functools.partial(pick_kernel, first),
         out_shape=jax.ShapeDtypeStruct((nodes, lists, piece, width), BF16),
         grid_spec=pltpu.PrefetchScalarGridSpec(
             num_scalar_prefetch=1,
             grid=(),
             in_specs=[vmem_spec()] * 2,
-            out_specs=pl.BlockSpec(memory_space=pltpu.HBM),
+            out_specs=hbm_spec(),
             scratch_shapes=[
                 pltpu.VMEM((nodes, lists, piece, width), BF16),
                 pltpu.SemaphoreType.DMA((8,)),
@@ -146,7 +152,7 @@
     tiles = blk // TILE
 
     def table(k):
-        return pl.BlockSpec((groups, 1, rows_in, width), lambda s, *_: (0, 2 * (first + s) + k, 0, 0))
+        return pl.BlockSpec((groups, 1, rows_in, width), lambda s, *_: (0, 2 * s + k, 0, 0))
 
     def chunk(i):
         return pl.BlockSpec((1, TILE, blk), lambda s, *_: (first + s, i, 0))
@@ -187,17 +193,17 @@
     lax.fori_loop(0, ret_ref.shape[0], one, 0)
 
 
-def sum_kernel(req, ret_ref, row_out, col_out):
+def sum_kernel(first, req, ret_ref, row_out, col_out):
     row_out[...] = jnp.zeros_like(row_out)
     col_out[...] = jnp.zeros_like(col_out)
-    add_parts(0, req, ret_ref, row_out, col_out)
-
-
-def sums(req, ret, blocks):
+    add_parts(2 * first, req, ret_ref, row_out, col_out)
+
+
+def sums(req, ret, blocks, first):
     piece, width = ret.shape[2:]
     shape = jax.ShapeDtypeStruct((blocks, piece, width), F32)
     return pl.pallas_call(
-        sum_kernel,
+        functools.partial(sum_kernel, first),
         out_shape=(shape, shape),
         grid_spec=pltpu.PrefetchScalarGridSpec(
             num_scalar_prefetch=1,
@@ -215,33 +221,65 @@
     )(req, ret)
 
 
-def update_kernel(first, req, ret_ref, rg, cg, rm, ra, cm, ca, rn, ran, cn, can, row_s, col_s):
-    row_s[...] = rg[...]
-    col_s[...] = cg[...]
-    add_parts(first, req, ret_ref, row_s, col_s)
-    for grads, master, accum, new, accum_out in ((row_s, rm, ra, rn, ran), (col_s, cm, ca, cn, can)):
-        grad = grads[...]
-        accum_new = accum[...] + grad * grad
-        accum_out[...] = accum_new
-        new[...] = master[...] - LEARN_RATE * grad * lax.rsqrt(accum_new)
+def update_kernel(
+    first, req, ret_hbm, rg, cg, rm, ra, cm, ca, rn, ran, cn, can, ret_ref, held, done, ret_sems, sems, out_sems
+):
+    lists = ret_hbm.shape[1]
+    tables = ((rg, rm, ra, rn, ran), (cg, cm, ca, cn, can))
+    parts, loads, stores = {}, {}, []
+    for side, refs in enumerate(tables):
+        for k in range(side, lists, 2):
+            parts[k] = pltpu.make_async_copy(ret_hbm.at[:, k], ret_ref.at[k], ret_sems.at[k])
+            parts[k].start()
+        for i in range(3):
+            at = 3 * side + i
+            loads[at] = pltpu.make_async_copy(refs[i], held.at[at], sems.at[at])
+            loads[at].start()
+    for side, refs in enumerate(tables):
+        at = 3 * side
+        loads[at].wait()
+        for k in range(side, lists, 2):
+            parts[k].wait()
+
+            def one(node, carry, k=k, at=at):
+                held[at, req[node, 2 * first + k]] += ret_ref[k, node].astype(F32)
+                return carry
+
+            lax.fori_loop(0, ret_hbm.shape[0], one, 0, unroll=4)
+        loads[at + 1].wait()
+        loads[at + 2].wait()
+        grad = held[at]
+        accum_new = held[at + 2] + grad * grad
+        done[2 * side + 1] = accum_new
+        done[2 * side] = held[at + 1] - LEARN_RATE * grad * lax.rsqrt(accum_new)
+        for i in range(2):
+            copy = pltpu.make_async_copy(
+                done.at[2 * side + i], refs[3 + i], out_sems.at[2 * side + i]
+            )
+            copy.start()
+            stores.append(copy)
+    for copy in stores:
+        copy.wait()
 
 
 def update(req, ret, row_grad, col_grad, row_master, row_accum, col_master, col_accum, first):
-    blocks, piece, width = row_master.shape
-    nodes, lists = ret.shape[:2]
     shape = jax.ShapeDtypeStruct(row_master.shape, F32)
-    rows = piece if piece % 16 else 16
-    table = pl.BlockSpec((blocks, rows, width), lambda i, *_: (0, i, 0))
     return pl.pallas_call(
         functools.partial(update_kernel, first),
         out_shape=(shape,) * 4,
         grid_spec=pltpu.PrefetchScalarGridSpec(
             num_scalar_prefetch=1,
-            grid=(piece // rows,),
-            in_specs=[pl.BlockSpec((nodes, lists, rows, width), lambda i, *_: (0, 0, i, 0))]
-            + [table] * 6,
-            out_specs=(table,) * 4,
-            scratch_shapes=[pltpu.VMEM((blocks, rows, width), F32)] * 2,
+            grid=(),
+            in_specs=[hbm_spec()] * 7,
+            out_specs=(hbm_spec(),) * 4,
+            scratch_shapes=[
+                pltpu.VMEM((ret.shape[1], ret.shape[0]) + ret.shape[2:], BF16),
+                pltpu.VMEM((6,) + row_master.shape, F32),
+                pltpu.VMEM((4,) + row_master.shape, F32),
+                pltpu.SemaphoreType.DMA((ret.shape[1],)),
+                pltpu.SemaphoreType.DMA((6,)),
+                pltpu.SemaphoreType.DMA((4,)),
+            ],
         ),
         compiler_params=params(),
         cost_estimate=pl.CostEstimate(
@@ -264,17 +302,18 @@
     blocks = row_master.shape[0]
     nodes = lax.axis_size(AXES)
     req = exchange(jnp.broadcast_to(pairs.reshape(1, 2 * slots), (nodes, 2 * slots)))
-    got = exchange(pick(req, row_master.astype(BF16), col_master.astype(BF16)))
-    lead = 1
-    back = items(pairs, live, got, counts, row_marginal, col_marginal, 0, lead)
-    back = exchange(back)
-    rest = items(pairs, live, got, counts, row_marginal, col_marginal, lead, slots - lead)
-    rest, back = lax.optimization_barrier((rest, back))
-    rest = exchange(rest)
-    row_grad, col_grad = sums(req, back, blocks)
-    return update(
-        req, rest, row_grad, col_grad, row_master, row_accum, col_master, col_accum, 2 * lead
-    )
+    row_low = row_master.astype(BF16)
+    col_low = col_master.astype(BF16)
+    lists = ((1, slots - 1), (0, 1))
+    got = [exchange(pick(req, row_low, col_low, *part)) for part in lists]
+    back = []
+    for part, rows in zip(lists, got):
+        work = items(pairs, live, rows, counts, row_marginal, col_marginal, *part)
+        if back:
+            work, back[-1] = lax.optimization_barrier((work, back[-1]))
+        back.append(exchange(work))
+    row_grad, col_grad = sums(req, back[0], blocks, 1)
+    return update(req, back[1], row_grad, col_grad, row_master, row_accum, col_master, col_accum, 0)
 
 
 def solution(mesh):

time: 194 us -> 191 us (0.985)
  waiting for transfers between devices: 135 us -> 129 us
  starting transfers between devices: 18.8 us -> 22.9 us
    all_to_all x4 -> x5, waiting for transfers between devices: 135 us -> 129 us  [exchange(): return lax.all_to_all(x, AXES, split_axis=0, concat_axis=0, tiled=True)]
    all_to_all x4 -> x5, starting transfers between devices: 18.8 us -> 22.9 us  [exchange(): return lax.all_to_all(x, AXES, split_axis=0, concat_axis=0, tiled=True)]
    pallas_call x2 -> x3, Pallas kernels: 6.58 us -> 8.66 us  [the longest x1 4.58 us: sums(): pl.pallas_call(functools.partial(sum_kernel, first), out_shape=(shape, sh...]
  transfers between devices with their start and end apart: 4 -> 5, of which waited for: 4 -> 5; matrix products, arithmetic and copies ran while one was open for 1% -> 1% of each run, Pallas kernels for 8% -> 14%
where the time goes in v3:
time: 191 us; the launch traced here: 190 us
  waiting for transfers between devices  129 us (68%)
  Pallas kernels  34.1 us (18%)
  starting transfers between devices  22.9 us (12%)
    all_to_all x5, waiting for transfers between devices, exchange(): return lax.all_to_all(x, AXES, split_axis=0, concat_axis=0, tiled=True)  129 us
    all_to_all x5, starting transfers between devices, exchange(): return lax.all_to_all(x, AXES, split_axis=0, concat_axis=0, tiled=True)  22.9 us
    pallas_call x2, Pallas kernels, items(): pl.pallas_call(functools.partial(item_kernel, first), out_shape=jax.Shape...  19.7 us
    pallas_call x1, Pallas kernels, update(): pl.pallas_call(functools.partial(update_kernel, first), out_shape=(shape,...  5.78 us
    pallas_call x1, Pallas kernels, sums(): pl.pallas_call(functools.partial(sum_kernel, first), out_shape=(shape, sh...  4.58 us
    pallas_call x2, Pallas kernels, pick(): pl.pallas_call(functools.partial(pick_kernel, first), out_shape=jax.Shape...  4.08 us
  transfers between devices with their start and end apart: 5, of which 5 were waited for; matrix products, arithmetic and copies ran while one was open for 1% of the time, Pallas kernels for 14%

profile of v3, /device:TPU:0, one launch (start us, length us, event | category | flops | bytes accessed | tf_op | source)
XLA Modules:
  0.0 190.1 jit_solution(4458600489564008952)
XLA Ops:
  0.6 0.0 copy-start.1
  0.6 0.9 copy.19.pairs
  1.5 0.1 broadcast_in_dim.7
  1.6 0.6 broadcast_in_dim.8
  2.2 7.3 %all-to-all-start = ((s32[32,1,6]{2,1,0:T(1,128)}), s32[32,1,6]{2,1,0:T(1,128)S(1)}, u32[]{:S(2)}, u32[]{:S(2)}) async-start(s32[32,1,6]{2,1,0:T(1,128)} %broadcast_in_dim.8), calls=%async_computation | async-start | bytes 32768 | tf_op jit(solution)/shard_map/all_to_all | solution.py:295
  9.5 1.3 convert_element_type.6.row_ref
  10.8 0.0 copy-done.1
  10.8 0.1 convert_element_type.7.col_ref
  10.9 5.7 %all-to-all-done = s32[32,1,6]{2,1,0:T(1,128)S(1)} async-done(((s32[32,1,6]{2,1,0:T(1,128)}), s32[32,1,6]{2,1,0:T(1,128)S(1)}, u32[]{:S(2)}, u32[]{:S(2)}) %all-to-all-start) | async-done | bytes 800 | tf_op jit(solution)/shard_map/all_to_all | solution.py:295
  16.6 2.2 %pick.3 = bf16[32,4,32,256]{3,2,1,0:T(8,128)(2,1)} custom-call(s32[32,6]{1,0:T(8,128)S(1)} %bitcast.1, bf16[32,32,256]{2,1,0:T(8,128)(2,1)S(1)} %convert_element_type.6.row_ref, bf16[32,32,256]{2,1,0:T(8,128)(2,1)S(1)} %convert_element_type.7.col_ref), custom_call_target="tpu_custom_call" | custom-call | bytes 3145728 | tf_op jit(solution)/shard_map/pick/pallas_call | solution.py:60
  18.8 3.5 %all-to-all-start.2 = ((bf16[32,4,32,256]{3,2,1,0:T(8,128)(2,1)}), bf16[32,4,32,256]{3,2,1,0:T(8,128)(2,1)}, u32[]{:S(2)}, u32[]{:S(2)}) async-start(bf16[32,4,32,256]{3,2,1,0:T(8,128)(2,1)} %pick.3), calls=%async_computation.2 | async-start | bytes 4194304 | tf_op jit(solution)/shard_map/all_to_all | solution.py:295
  22.3 0.0 copy-done
  22.3 1.9 pick.2
  24.2 46.9 %all-to-all-done.2.rows_ref.cols_ref = bf16[32,4,32,256]{3,2,1,0:T(8,128)(2,1)} async-done(((bf16[32,4,32,256]{3,2,1,0:T(8,128)(2,1)}), bf16[32,4,32,256]{3,2,1,0:T(8,128)(2,1)}, u32[]{:S(2)}, u32[]{:S(2)}) %all-to-all-start.2) | async-done | bytes 2097184 | tf_op jit(solution)/shard_map/all_to_all | solution.py:295
  71.1 4.1 %all-to-all-start.1 = ((bf16[32,2,32,256]{3,2,1,0:T(8,128)(2,1)}), bf16[32,2,32,256]{3,2,1,0:T(8,128)(2,1)}, u32[]{:S(2)}, u32[]{:S(2)}) async-start(bf16[32,2,32,256]{3,2,1,0:T(8,128)(2,1)} %pick.2), calls=%async_computation.1 | async-start | bytes 2097152 | tf_op jit(solution)/shard_map/all_to_all | solution.py:295
  75.8 11.8 %items.3 = bf16[32,4,32,256]{3,2,1,0:T(8,128)(2,1)} custom-call(s32[3,2]{1,0:T(4,128)} %copy-done.2, s32[1]{0:T(128)S(6)} %copy.22.live, bf16[32,4,32,256]{3,2,1,0:T(8,128)(2,1)} %all-to-all-done.2.rows_ref.cols_ref, bf16[32,4,32,256]{3,2,1,0:T(8,128)(2,1)} %all-to-all-done.2.rows_ref.cols_ref, s32[3,1024,1024]{2,1,0:T(8,128)} %refs_3_.3, ...), custom_call_target="tpu_custom_call" | custom-call | flops 3221225472 | bytes 12582912 | tf_op jit(solution)/shard_map/items/pallas_call | solution.py:160
  87.6 13.8 %all-to-all-done.1.rows_ref.cols_ref = bf16[32,2,32,256]{3,2,1,0:T(8,128)(2,1)} async-done(((bf16[32,2,32,256]{3,2,1,0:T(8,128)(2,1)}), bf16[32,2,32,256]{3,2,1,0:T(8,128)(2,1)}, u32[]{:S(2)}, u32[]{:S(2)}) %all-to-all-start.1) | async-done | bytes 1048608 | tf_op jit(solution)/shard_map/all_to_all | solution.py:295
  101.4 3.7 %all-to-all-start.3 = ((bf16[32,4,32,256]{3,2,1,0:T(8,128)(2,1)}), bf16[32,4,32,256]{3,2,1,0:T(8,128)(2,1)}, u32[]{:S(2)}, u32[]{:S(2)}) async-start(bf16[32,4,32,256]{3,2,1,0:T(8,128)(2,1)} %items.3), calls=%async_computation.3 | async-start | bytes 4194304 | tf_op jit(solution)/shard_map/all_to_all | solution.py:295
  105.1 7.9 %items.2 = bf16[32,2,32,256]{3,2,1,0:T(8,128)(2,1)} custom-call(s32[3,2]{1,0:T(4,128)} %copy-done.2, s32[1]{0:T(128)S(6)} %copy.22.live, bf16[32,2,32,256]{3,2,1,0:T(8,128)(2,1)} %all-to-all-done.1.rows_ref.cols_ref, bf16[32,2,32,256]{3,2,1,0:T(8,128)(2,1)} %all-to-all-done.1.rows_ref.cols_ref, s32[3,1024,1024]{2,1,0:T(8,128)} %refs_3_.3, ...), custom_call_target="tpu_custom_call" | custom-call | flops 1610612736 | bytes 6291456 | tf_op jit(solution)/shard_map/items/pallas_call | solution.py:160
  113.0 40.9 %all-to-all-done.3.ret_ref = bf16[32,4,32,256]{3,2,1,0:T(8,128)(2,1)} async-done(((bf16[32,4,32,256]{3,2,1,0:T(8,128)(2,1)}), bf16[32,4,32,256]{3,2,1,0:T(8,128)(2,1)}, u32[]{:S(2)}, u32[]{:S(2)}) %all-to-all-start.3) | async-done | bytes 2097184 | tf_op jit(solution)/shard_map/all_to_all | solution.py:295
  153.9 4.2 %all-to-all-start.4 = ((bf16[32,2,32,256]{3,2,1,0:T(8,128)(2,1)}), bf16[32,2,32,256]{3,2,1,0:T(8,128)(2,1)}, u32[]{:S(2)}, u32[]{:S(2)}) async-start(bf16[32,2,32,256]{3,2,1,0:T(8,128)(2,1)} %items.2), calls=%async_computation.4 | async-start | bytes 2097152 | tf_op jit(solution)/shard_map/all_to_all | solution.py:295
  158.1 4.6 %sums.1 = (f32[32,32,256]{2,1,0:T(8,128)}, f32[32,32,256]{2,1,0:T(8,128)}) custom-call(s32[32,6]{1,0:T(8,128)} %bitcast.3, bf16[32,4,32,256]{3,2,1,0:T(8,128)(2,1)} %all-to-all-done.3.ret_ref), custom_call_target="tpu_custom_call" | custom-call | flops 1048576 | bytes 4194304 | tf_op jit(solution)/shard_map/sums/pallas_call | solution.py:205
  162.7 21.6 %all-to-all-done.4.ret_hbm = bf16[32,2,32,256]{3,2,1,0:T(8,128)(2,1)} async-done(((bf16[32,2,32,256]{3,2,1,0:T(8,128)(2,1)}), bf16[32,2,32,256]{3,2,1,0:T(8,128)(2,1)}, u32[]{:S(2)}, u32[]{:S(2)}) %all-to-all-start.4) | async-done | bytes 1048608 | tf_op jit(solution)/shard_map/all_to_all | solution.py:295
  184.3 5.8 %update.1 = (f32[32,32,256]{2,1,0:T(8,128)}, f32[32,32,256]{2,1,0:T(8,128)}, f32[32,32,256]{2,1,0:T(8,128)}, f32[32,32,256]{2,1,0:T(8,128)}) custom-call(s32[32,6]{1,0:T(8,128)} %bitcast.4, bf16[32,2,32,256]{3,2,1,0:T(8,128)(2,1)} %all-to-all-done.4.ret_hbm, f32[32,32,256]{2,1,0:T(8,128)} %get-tuple-element.10.rg, f32[32,32,256]{2,1,0:T(8,128)} %get-tuple-element.11.cg, ...), custom_call_target="tpu_custom_call" | custom-call | flops 2097152 | bytes 11534336 | tf_op jit(solution)/shard_map/update/pallas_call | solution.py:267
  (3 shorter events, 0.0 us)
Async XLA Ops:
  0.6 10.2 %copy-start.1 = (f32[32,32,256]{2,1,0:T(8,128)S(1)}, f32[32,32,256]{2,1,0:T(8,128)}, u32[]{:S(2)}) copy-start(f32[32,32,256]{2,1,0:T(8,128)} %cm.1) | copy-start | bytes 3145732
  1.5 17.3 %copy-start.2 = (s32[3,2]{1,0:T(4,128)}, s32[3,2]{1,0:T(4,128)S(1)}, u32[]{:S(2)}) copy-start(s32[3,2]{1,0:T(4,128)S(1)} %copy.19.pairs) | copy-start | bytes 76
  2.2 14.4 %all-to-all-start = ((s32[32,1,6]{2,1,0:T(1,128)}), s32[32,1,6]{2,1,0:T(1,128)S(1)}, u32[]{:S(2)}, u32[]{:S(2)}) async-start(s32[32,1,6]{2,1,0:T(1,128)} %broadcast_in_dim.8), calls=%async_computation | async-start | bytes 32768 | tf_op jit(solution)/shard_map/all_to_all | solution.py:295
  16.6 5.8 %copy-start = (s32[32,1,6]{2,1,0:T(1,128)}, s32[32,1,6]{2,1,0:T(1,128)S(1)}, u32[]{:S(2)}) copy-start(s32[32,1,6]{2,1,0:T(1,128)S(1)} %all-to-all-done) | copy-start | bytes 2308
  18.8 52.2 %all-to-all-start.2 = ((bf16[32,4,32,256]{3,2,1,0:T(8,128)(2,1)}), bf16[32,4,32,256]{3,2,1,0:T(8,128)(2,1)}, u32[]{:S(2)}, u32[]{:S(2)}) async-start(bf16[32,4,32,256]{3,2,1,0:T(8,128)(2,1)} %pick.3), calls=%async_computation.2 | async-start | bytes 4194304 | tf_op jit(solution)/shard_map/all_to_all | solution.py:295
  71.1 30.3 %all-to-all-start.1 = ((bf16[32,2,32,256]{3,2,1,0:T(8,128)(2,1)}), bf16[32,2,32,256]{3,2,1,0:T(8,128)(2,1)}, u32[]{:S(2)}, u32[]{:S(2)}) async-start(bf16[32,2,32,256]{3,2,1,0:T(8,128)(2,1)} %pick.2), calls=%async_computation.1 | async-start | bytes 2097152 | tf_op jit(solution)/shard_map/all_to_all | solution.py:295
  101.4 52.5 %all-to-all-start.3 = ((bf16[32,4,32,256]{3,2,1,0:T(8,128)(2,1)}), bf16[32,4,32,256]{3,2,1,0:T(8,128)(2,1)}, u32[]{:S(2)}, u32[]{:S(2)}) async-start(bf16[32,4,32,256]{3,2,1,0:T(8,128)(2,1)} %items.3), calls=%async_computation.3 | async-start | bytes 4194304 | tf_op jit(solution)/shard_map/all_to_all | solution.py:295
  153.9 30.4 %all-to-all-start.4 = ((bf16[32,2,32,256]{3,2,1,0:T(8,128)(2,1)}), bf16[32,2,32,256]{3,2,1,0:T(8,128)(2,1)}, u32[]{:S(2)}, u32[]{:S(2)}) async-start(bf16[32,2,32,256]{3,2,1,0:T(8,128)(2,1)} %items.2), calls=%async_computation.4 | async-start | bytes 2097152 | tf_op jit(solution)/shard_map/all_to_all | solution.py:295

commit v4 on v3

v4 whole, which is shorter than its diff:
```python
import functools

import jax
import jax.numpy as jnp
from jax import lax
from jax.experimental import pallas as pl
from jax.experimental.pallas import tpu as pltpu
from jax.sharding import PartitionSpec as P

LOG_TOTAL = 14.3
LEARN_RATE = 0.05
AXES = ("rows", "cols")
TILE = 512
JOINED = 256
VMEM_LIMIT = 65280 * 1024

BF16 = jnp.bfloat16
F32 = jnp.float32


def vmem_spec():
    return pl.BlockSpec(memory_space=pltpu.VMEM)


def hbm_spec():
    return pl.BlockSpec(memory_space=pltpu.HBM)


def params():
    return pltpu.CompilerParams(vmem_limit_bytes=VMEM_LIMIT)


def pick_kernel(first, req, row_ref, col_ref, out_ref, held, sems):
    nodes, lists = out_ref.shape[:2]
    chunks = sems.shape[0]
    span = nodes // chunks
    copies = []
    for chunk in range(chunks):

        def one(i, carry, base=chunk * span):
            node = base + i
            for k in range(0, lists, 2):
                held[node, k] = row_ref[req[node, 0, first + k // 2]]
                held[node, k + 1] = col_ref[req[node, 1, first + k // 2]]
            return carry

        lax.fori_loop(0, span, one, 0)
        part = pl.ds(chunk * span, span)
        copy = pltpu.make_async_copy(held.at[part], out_ref.at[part], sems.at[chunk])
        copy.start()
        copies.append(copy)
    for copy in copies:
        copy.wait()


def pick(req, rows, cols, first, count):
    nodes = req.shape[0]
    lists = 2 * count
    piece, width = rows.shape[1:]
    return pl.pallas_call(
        functools.partial(pick_kernel, first),
        out_shape=jax.ShapeDtypeStruct((nodes, lists, piece, width), BF16),
        grid_spec=pltpu.PrefetchScalarGridSpec(
            num_scalar_prefetch=1,
            grid=(),
            in_specs=[vmem_spec()] * 2,
            out_specs=hbm_spec(),
            scratch_shapes=[
                pltpu.VMEM((nodes, lists, piece, width), BF16),
                pltpu.SemaphoreType.DMA((8,)),
            ],
        ),
        compiler_params=pltpu.CompilerParams(vmem_limit_bytes=VMEM_LIMIT if first else VMEM_LIMIT // 4),
        cost_estimate=pl.CostEstimate(
            flops=0,
            bytes_accessed=4 * rows.size + nodes * lists * piece * width * 2,
            transcendentals=0,
        ),
        name="pick",
    )(req, rows, cols)


def prepare_kernel(pairs, live, counts_ref, rm_ref, cm_ref, bias_ref, weight_ref):
    slot = pl.program_id(0)
    size, blk = counts_ref.shape[1:]

    @pl.when(slot < live[0])
    def _():
        at = pl.multiple_of(pl.program_id(1) * size, size)
        col_log = jnp.log(cm_ref[pl.ds(pairs[slot, 1], 1), :].astype(F32))
        row_log = jnp.log(rm_ref[pl.ds(pairs[slot, 0], 1), pl.ds(at, size)].astype(F32)) - LOG_TOTAL
        row_log = jnp.transpose(jnp.broadcast_to(row_log, (8, size)))[:, :1]
        scale = 1.0 / (blk**0.5)
        counts = counts_ref[0].astype(F32)
        seen = jnp.maximum(counts, 1.0)
        bias_ref[0] = (row_log + col_log) - jnp.log(seen)
        weight = 0.1 * scale + (0.25 * scale) * (seen * lax.rsqrt(seen))
        weight_ref[0] = jnp.where(counts > 0.0, weight, 0.0)


def prepare(pairs, live, counts, row_marginal, col_marginal):
    slots, blk, _ = counts.shape
    size = blk // 4
    tile = pl.BlockSpec((1, size, blk), lambda s, i, *_: (s, i, 0))
    whole = pl.BlockSpec(row_marginal.shape, lambda s, i, *_: (0, 0))
    shape = jax.ShapeDtypeStruct(counts.shape, F32)
    return pl.pallas_call(
        prepare_kernel,
        out_shape=(shape, shape),
        grid_spec=pltpu.PrefetchScalarGridSpec(
            num_scalar_prefetch=2,
            grid=(slots, blk // size),
            in_specs=[tile, whole, whole],
            out_specs=(tile, tile),
        ),
        compiler_params=params(),
        cost_estimate=pl.CostEstimate(
            flops=10 * counts.size, bytes_accessed=12 * counts.size, transcendentals=2 * counts.size
        ),
        name="prepare",
    )(pairs, live, counts, row_marginal, col_marginal)


def item_kernel(first, live, rows_ref, cols_ref, bias_ref, weight_ref, *refs):
    out_ref, acc_s = refs[-2:]
    slot = first + pl.program_id(0)
    step = pl.program_id(1)
    groups, _, piece, width = rows_ref.shape
    blk = groups * piece
    span = TILE // piece
    alive = slot < live[0]

    @pl.when(alive)
    def _():
        cols = cols_ref[...].reshape(blk, width)
        rows = rows_ref[pl.ds(step * span, span)].reshape(TILE, width)
        logits = lax.dot_general(rows, cols, (((1,), (1,)), ((), ())), preferred_element_type=F32)
        spread = logits + bias_ref[0]
        weight = weight_ref[0]
        scale = 1.0 / (blk**0.5)
        unseen = (0.5 * scale) * jnp.tanh(0.5 * spread) + 0.5 * scale
        delta = jnp.where(weight > 0.0, weight * spread, unseen).astype(BF16)
        row_part = jnp.dot(delta, cols, preferred_element_type=F32).astype(BF16)
        out_ref[pl.ds(step * span, span), 0] = row_part.reshape(span, piece, width)
        part = lax.dot_general(rows, delta, (((0,), (0,)), ((), ())), preferred_element_type=F32)

        @pl.when(step == 0)
        def _():
            acc_s[...] = part

        @pl.when(step == pl.num_programs(1) - 1)
        def _():
            total = jnp.transpose(acc_s[...] + part)
            out_ref[:, 1] = total.astype(BF16).reshape(groups, piece, width)

    @pl.when(jnp.logical_not(alive) & (step == 0))
    def _():
        out_ref[...] = jnp.zeros_like(out_ref)


def join(got):
    nodes, lists, piece, width = got.shape
    if piece % 16 == 0:
        return got
    got = got.transpose(1, 0, 2, 3).reshape(lists, nodes * piece // JOINED, JOINED, width)
    return got.transpose(1, 0, 2, 3)


def cut(out, nodes, piece):
    groups, lists, rows, width = out.shape
    if rows == piece:
        return out
    out = out.transpose(1, 0, 2, 3).reshape(lists, nodes, piece, width)
    return out.transpose(1, 0, 2, 3)


def items(live, got, bias, weight, first, count, into=None):
    width = got.shape[3]
    slots, blk, _ = bias.shape
    got = join(got)
    groups, _, rows_in, _ = got.shape
    steps = blk // TILE
    assert steps == 2

    def table(k):
        return pl.BlockSpec((groups, 1, rows_in, width), lambda s, i, *_: (0, 2 * s + k, 0, 0))

    tile = pl.BlockSpec((1, TILE, blk), lambda s, i, *_: (first + s, i, 0))
    earlier = () if into is None else (into,)
    return pl.pallas_call(
        functools.partial(item_kernel, first),
        out_shape=jax.ShapeDtypeStruct((groups, 2 * slots, rows_in, width), BF16),
        grid_spec=pltpu.PrefetchScalarGridSpec(
            num_scalar_prefetch=1,
            grid=(count, steps),
            in_specs=[table(0), table(1), tile, tile] + [hbm_spec()] * len(earlier),
            out_specs=pl.BlockSpec((groups, 2, rows_in, width), lambda s, i, *_: (0, first + s, 0, 0)),
            scratch_shapes=[pltpu.VMEM((width, blk), F32)],
        ),
        input_output_aliases={5: 0} if earlier else {},
        compiler_params=params(),
        cost_estimate=pl.CostEstimate(
            flops=6 * count * blk * blk * width,
            bytes_accessed=count * (blk * blk * 8 + 4 * blk * width * 2),
            transcendentals=count * blk * blk,
        ),
        name="items",
    )(live, got, got, bias, weight, *earlier)


def update_kernel(req, ret_hbm, rm, ra, cm, ca, rn, ran, cn, can, ret_ref, grads, held, done, ret_sems, sems, out_sems):
    lists = ret_hbm.shape[1]
    tables = ((rm, ra, rn, ran), (cm, ca, cn, can))
    parts, loads, stores = {}, {}, []
    for side, refs in enumerate(tables):
        for k in range(side, lists, 2):
            parts[k] = pltpu.make_async_copy(ret_hbm.at[:, k], ret_ref.at[k], ret_sems.at[k])
            parts[k].start()
        for i in range(2):
            at = 2 * side + i
            loads[at] = pltpu.make_async_copy(refs[i], held.at[at], sems.at[at])
            loads[at].start()
    grads[...] = jnp.zeros_like(grads)
    for side, refs in enumerate(tables):
        for k in range(side, lists, 2):
            parts[k].wait()

            def one(node, carry, k=k, side=side):
                grads[side, req[node, side, k // 2]] += ret_ref[k, node].astype(F32)
                return carry

            lax.fori_loop(0, ret_hbm.shape[0], one, 0, unroll=4)
        at = 2 * side
        loads[at].wait()
        loads[at + 1].wait()
        grad = grads[side]
        accum_new = held[at + 1] + grad * grad
        done[at + 1] = accum_new
        done[at] = held[at] - LEARN_RATE * grad * lax.rsqrt(accum_new)
        for i in range(2):
            copy = pltpu.make_async_copy(done.at[at + i], refs[2 + i], out_sems.at[at + i])
            copy.start()
            stores.append(copy)
    for copy in stores:
        copy.wait()


def update(req, ret, row_master, row_accum, col_master, col_accum):
    shape = jax.ShapeDtypeStruct(row_master.shape, F32)
    nodes, lists = ret.shape[:2]
    return pl.pallas_call(
        update_kernel,
        out_shape=(shape,) * 4,
        grid_spec=pltpu.PrefetchScalarGridSpec(
            num_scalar_prefetch=1,
            grid=(),
            in_specs=[hbm_spec()] * 5,
            out_specs=(hbm_spec(),) * 4,
            scratch_shapes=[
                pltpu.VMEM((lists, nodes) + ret.shape[2:], BF16),
                pltpu.VMEM((2,) + row_master.shape, F32),
                pltpu.VMEM((4,) + row_master.shape, F32),
                pltpu.VMEM((4,) + row_master.shape, F32),
                pltpu.SemaphoreType.DMA((lists,)),
                pltpu.SemaphoreType.DMA((4,)),
                pltpu.SemaphoreType.DMA((4,)),
            ],
        ),
        compiler_params=params(),
        cost_estimate=pl.CostEstimate(
            flops=8 * row_master.size + ret.size,
            bytes_accessed=ret.size * 2 + 32 * row_master.size,
            transcendentals=2 * row_master.size,
        ),
        name="update",
    )(req, ret, row_master, row_accum, col_master, col_accum)


def exchange(x):
    return lax.all_to_all(x, AXES, split_axis=0, concat_axis=0, tiled=True)


def body(
    row_master, row_accum, col_master, col_accum, pairs, live, counts, row_marginal, col_marginal
):
    slots = pairs.shape[0]
    nodes = lax.axis_size(AXES)
    req = exchange(jnp.broadcast_to(pairs.T[None], (nodes, 2, slots)))
    row_low = row_master.astype(BF16)
    col_low = col_master.astype(BF16)
    last = slots - 1
    first_got = exchange(pick(req, row_low, col_low, 0, last))
    bias, weight = prepare(pairs, live, counts, row_marginal, col_marginal)
    picked = pick(req, row_low, col_low, last, 1)
    picked, bias, weight = lax.optimization_barrier((picked, bias, weight))
    last_got = exchange(picked)
    parts = items(live, first_got, bias, weight, 0, last)
    parts = items(live, last_got, bias, weight, last, 1, parts)
    back = exchange(cut(parts, nodes, row_master.shape[1]))
    return update(req, back, row_master, row_accum, col_master, col_accum)


def solution(mesh):
    table = P(None, AXES, None)
    return jax.shard_map(
        body,
        mesh=mesh,
        in_specs=(
            table,
            table,
            table,
            table,
            P(AXES, None),
            P(AXES),
            P(AXES, None, None),
            P(),
            P(),
        ),
        out_specs=(table,) * 4,
        check_vma=False,
    )
```

time: 191 us -> 190 us (level)
  waiting for transfers between devices: 129 us -> 45.5 us
  blocking collectives: 0 us -> 74.7 us
  Pallas kernels: 34.1 us -> 47.5 us
  starting transfers between devices: 22.9 us -> 14.9 us
    all_to_all x5 -> x3, waiting for transfers between devices: 129 us -> 45.5 us  [exchange(): return lax.all_to_all(x, AXES, split_axis=0, concat_axis=0, tiled=True)]
    all_to_all x0 -> x1, blocking collectives: none -> 74.7 us  [exchange(): return lax.all_to_all(x, AXES, split_axis=0, concat_axis=0, tiled=True)]
    pallas_call x2, Pallas kernels: 10.4 us -> 24.2 us  [the longest x1 18.1 us: prepare(): pl.pallas_call(prepare_kernel, out_shape=(shape, shape), grid_spec=pltpu....]
    all_to_all x5 -> x3, starting transfers between devices: 22.9 us -> 14.9 us  [exchange(): return lax.all_to_all(x, AXES, split_axis=0, concat_axis=0, tiled=True)]
    pallas_call x2, Pallas kernels: 19.7 us -> 17.3 us  [items(): pl.pallas_call(functools.partial(item_kernel, first), out_shape=jax.Shape...]
  transfers between devices with their start and end apart: 5 -> 3, of which waited for: 5 -> 3; matrix products, arithmetic and copies ran while one was open for 1% -> 2% of each run, Pallas kernels for 14% -> 17%
where the time goes in v4:
time: 190 us; the launch traced here: 189 us
  blocking collectives  74.7 us (39%)
  Pallas kernels  47.5 us (25%)
  waiting for transfers between devices  45.5 us (24%)
  starting transfers between devices  14.9 us (8%)
  other arithmetic  2.78 us (1%)
  local copies, waits for them, and re-layouts  1.99 us (1%)
    all_to_all x1, blocking collectives, exchange(): return lax.all_to_all(x, AXES, split_axis=0, concat_axis=0, tiled=True)  74.7 us
    all_to_all x3, waiting for transfers between devices, exchange(): return lax.all_to_all(x, AXES, split_axis=0, concat_axis=0, tiled=True)  45.5 us
    pallas_call x1, Pallas kernels, prepare(): pl.pallas_call(prepare_kernel, out_shape=(shape, shape), grid_spec=pltpu....  18.1 us
    pallas_call x2, Pallas kernels, items(): pl.pallas_call(functools.partial(item_kernel, first), out_shape=jax.Shape...  17.3 us
    all_to_all x3, starting transfers between devices, exchange(): return lax.all_to_all(x, AXES, split_axis=0, concat_axis=0, tiled=True)  14.9 us
    pallas_call x1, Pallas kernels, update(): pl.pallas_call(update_kernel, out_shape=(shape,) * 4, grid_spec=pltpu.Pre...  6.05 us
    pallas_call x2, Pallas kernels, pick(): pl.pallas_call(functools.partial(pick_kernel, first), out_shape=jax.Shape...  5.96 us
  transfers between devices with their start and end apart: 3, of which 3 were waited for; matrix products, arithmetic and copies ran while one was open for 2% of the time, Pallas kernels for 17%

profile of v4, /device:TPU:0, one launch (start us, length us, event | category | flops | bytes accessed | tf_op | source)
XLA Modules:
  0.0 188.7 jit_solution(166538832973836654)
XLA Ops:
  0.6 1.3 broadcast_in_dim.2
  1.9 7.3 %all-to-all-start = ((s32[32,2,3]{2,1,0:T(2,128)}), s32[32,2,3]{2,1,0:T(2,128)S(1)}, u32[]{:S(2)}, u32[]{:S(2)}) async-start(s32[32,2,3]{2,1,0:T(2,128)} %broadcast_in_dim.2), calls=%async_computation | async-start | bytes 65536 | tf_op jit(solution)/shard_map/all_to_all | solution.py:280
  9.2 1.3 convert_element_type.6.row_ref
  10.5 0.0 copy-start
  10.6 1.5 convert_element_type.7.col_ref
  12.1 0.0 copy-start.1
  12.1 0.0 copy-start.3
  12.1 4.4 %all-to-all-done.req = s32[32,2,3]{2,1,0:T(2,128)S(1)} async-done(((s32[32,2,3]{2,1,0:T(2,128)}), s32[32,2,3]{2,1,0:T(2,128)S(1)}, u32[]{:S(2)}, u32[]{:S(2)}) %all-to-all-start) | async-done | bytes 800 | tf_op jit(solution)/shard_map/all_to_all | solution.py:280
  16.5 2.5 %pick.3 = bf16[32,4,32,256]{3,2,1,0:T(8,128)(2,1)} custom-call(s32[32,2,3]{2,1,0:T(2,128)S(1)} %all-to-all-done.req, bf16[32,32,256]{2,1,0:T(8,128)(2,1)S(1)} %convert_element_type.6.row_ref, bf16[32,32,256]{2,1,0:T(8,128)(2,1)S(1)} %convert_element_type.7.col_ref), custom_call_target="tpu_custom_call" | custom-call | bytes 3145728 | tf_op jit(solution)/shard_map/pick/pallas_call | solution.py:60
  19.0 0.0 copy-done
  19.0 0.0 copy-done.1
  19.1 0.0 copy-done.2
  19.1 3.5 %all-to-all-start.2 = ((bf16[32,4,32,256]{3,2,1,0:T(8,128)(2,1)}), bf16[32,4,32,256]{3,2,1,0:T(8,128)(2,1)}, u32[]{:S(2)}, u32[]{:S(2)}) async-start(bf16[32,4,32,256]{3,2,1,0:T(8,128)(2,1)} %pick.3), calls=%async_computation.2 | async-start | bytes 4194304 | tf_op jit(solution)/shard_map/all_to_all | solution.py:280
  22.6 0.0 copy-done.3
  22.6 0.7 copy.14.pairs
  23.9 18.1 %prepare.1 = (f32[3,1024,1024]{2,1,0:T(8,128)}, f32[3,1024,1024]{2,1,0:T(8,128)}) custom-call(s32[3,2]{1,0:T(4,128)} %copy.14.pairs, s32[1]{0:T(128)S(6)} %copy.16.live, s32[3,1024,1024]{2,1,0:T(8,128)} %counts_ref.1, s32[32,1024]{1,0:T(8,128)} %rm_ref.1, s32[32,1024]{1,0:T(8,128)} %cm_ref.1), custom_call_target="tpu_custom_call" | custom-call | flops 31457280 | bytes 37748736 | tf_op jit(solution)/shard_map/prepare/pallas_call | solution.py:107
  42.0 3.4 %pick.2 = bf16[32,2,32,256]{3,2,1,0:T(8,128)(2,1)} custom-call(s32[32,2,3]{2,1,0:T(2,128)} %copy-done.2, bf16[32,32,256]{2,1,0:T(8,128)(2,1)} %copy-done, bf16[32,32,256]{2,1,0:T(8,128)(2,1)} %copy-done.1), custom_call_target="tpu_custom_call" | custom-call | bytes 2097152 | tf_op jit(solution)/shard_map/pick/pallas_call | solution.py:60
  45.5 25.8 %all-to-all-done.2.rows_ref.cols_ref = bf16[32,4,32,256]{3,2,1,0:T(8,128)(2,1)} async-done(((bf16[32,4,32,256]{3,2,1,0:T(8,128)(2,1)}), bf16[32,4,32,256]{3,2,1,0:T(8,128)(2,1)}, u32[]{:S(2)}, u32[]{:S(2)}) %all-to-all-start.2) | async-done | bytes 2097184 | tf_op jit(solution)/shard_map/all_to_all | solution.py:280
  71.3 4.1 %all-to-all-start.1 = ((bf16[32,2,32,256]{3,2,1,0:T(8,128)(2,1)}), bf16[32,2,32,256]{3,2,1,0:T(8,128)(2,1)}, u32[]{:S(2)}, u32[]{:S(2)}) async-start(bf16[32,2,32,256]{3,2,1,0:T(8,128)(2,1)} %pick.2), calls=%async_computation.1 | async-start | bytes 2097152 | tf_op jit(solution)/shard_map/all_to_all | solution.py:280
  75.4 11.0 %items.2.refs_0_ = bf16[32,6,32,256]{3,2,1,0:T(8,128)(2,1)} custom-call(s32[1]{0:T(128)S(6)} %copy.16.live, bf16[32,4,32,256]{3,2,1,0:T(8,128)(2,1)} %all-to-all-done.2.rows_ref.cols_ref, bf16[32,4,32,256]{3,2,1,0:T(8,128)(2,1)} %all-to-all-done.2.rows_ref.cols_ref, f32[3,1024,1024]{2,1,0:T(8,128)} %get-tuple-element.12.bias_ref, ...), custom_call_target="tpu_custom_call" | custom-call | flops 3221225472 | bytes 20971520 | tf_op jit(solution)/shard_map/items/pallas_call | solution.py:190
  86.4 15.3 %all-to-all-done.1.rows_ref.cols_ref = bf16[32,2,32,256]{3,2,1,0:T(8,128)(2,1)} async-done(((bf16[32,2,32,256]{3,2,1,0:T(8,128)(2,1)}), bf16[32,2,32,256]{3,2,1,0:T(8,128)(2,1)}, u32[]{:S(2)}, u32[]{:S(2)}) %all-to-all-start.1) | async-done | bytes 1048608 | tf_op jit(solution)/shard_map/all_to_all | solution.py:280
  101.6 6.4 %items.3 = bf16[32,6,32,256]{3,2,1,0:T(8,128)(2,1)} custom-call(s32[1]{0:T(128)S(6)} %copy.16.live, bf16[32,2,32,256]{3,2,1,0:T(8,128)(2,1)} %all-to-all-done.1.rows_ref.cols_ref, bf16[32,2,32,256]{3,2,1,0:T(8,128)(2,1)} %all-to-all-done.1.rows_ref.cols_ref, f32[3,1024,1024]{2,1,0:T(8,128)} %get-tuple-element.12.bias_ref, ...), custom_call_target="tpu_custom_call", output_to_operand_aliasing={{}: (5, {})} | custom-call | flops 1610612736 | bytes 10485760 | tf_op jit(solution)/shard_map/items/pallas_call | solution.py:190
  108.0 74.7 %all_to_all.20.ret_hbm = bf16[32,6,32,256]{3,2,1,0:T(8,128)(2,1)} all-to-all(bf16[32,6,32,256]{3,2,1,0:T(8,128)(2,1)} %items.3), channel_id=1, replica_groups=mesh['rows'=8,'cols'=4] {'rows','cols'}, dimensions={0} | all-to-all | bytes 6291456 | tf_op jit(solution)/shard_map/all_to_all | solution.py:280
  182.7 6.0 %update.1 = (f32[32,32,256]{2,1,0:T(8,128)}, f32[32,32,256]{2,1,0:T(8,128)}, f32[32,32,256]{2,1,0:T(8,128)}, f32[32,32,256]{2,1,0:T(8,128)}) custom-call(s32[32,2,3]{2,1,0:T(2,128)} %copy-done.2, bf16[32,6,32,256]{3,2,1,0:T(8,128)(2,1)} %all_to_all.20.ret_hbm, f32[32,32,256]{2,1,0:T(8,128)} %rm.1, f32[32,32,256]{2,1,0:T(8,128)} %ra.1, f32[32,32,256]{2,1,0:T(8,128)} %cm.1, ...), custom_call_target="tpu_custom_call" | custom-call | flops 3670016 | bytes 11534336 | tf_op jit(solution)/shard_map/update/pallas_call | solution.py:251
  (1 shorter events, 0.0 us)
Async XLA Ops:
  1.9 14.6 %all-to-all-start = ((s32[32,2,3]{2,1,0:T(2,128)}), s32[32,2,3]{2,1,0:T(2,128)S(1)}, u32[]{:S(2)}, u32[]{:S(2)}) async-start(s32[32,2,3]{2,1,0:T(2,128)} %broadcast_in_dim.2), calls=%async_computation | async-start | bytes 65536 | tf_op jit(solution)/shard_map/all_to_all | solution.py:280
  10.5 8.5 %copy-start = (bf16[32,32,256]{2,1,0:T(8,128)(2,1)}, bf16[32,32,256]{2,1,0:T(8,128)(2,1)S(1)}, u32[]{:S(2)}) copy-start(bf16[32,32,256]{2,1,0:T(8,128)(2,1)S(1)} %convert_element_type.6.row_ref) | copy-start | bytes 1572868
  12.1 7.0 %copy-start.1 = (bf16[32,32,256]{2,1,0:T(8,128)(2,1)}, bf16[32,32,256]{2,1,0:T(8,128)(2,1)S(1)}, u32[]{:S(2)}) copy-start(bf16[32,32,256]{2,1,0:T(8,128)(2,1)S(1)} %convert_element_type.7.col_ref) | copy-start | bytes 1572868
  12.1 10.5 %copy-start.3 = (s32[3,2]{0,1:T(2,128)S(1)}, s32[3,2]{0,1:T(2,128)}, u32[]{:S(2)}) copy-start(s32[3,2]{0,1:T(2,128)} %param.13) | copy-start | bytes 76
  16.5 2.6 %copy-start.2 = (s32[32,2,3]{2,1,0:T(2,128)}, s32[32,2,3]{2,1,0:T(2,128)S(1)}, u32[]{:S(2)}) copy-start(s32[32,2,3]{2,1,0:T(2,128)S(1)} %all-to-all-done.req) | copy-start | bytes 2308
  19.1 52.2 %all-to-all-start.2 = ((bf16[32,4,32,256]{3,2,1,0:T(8,128)(2,1)}), bf16[32,4,32,256]{3,2,1,0:T(8,128)(2,1)}, u32[]{:S(2)}, u32[]{:S(2)}) async-start(bf16[32,4,32,256]{3,2,1,0:T(8,128)(2,1)} %pick.3), calls=%async_computation.2 | async-start | bytes 4194304 | tf_op jit(solution)/shard_map/all_to_all | solution.py:280
  71.3 30.3 %all-to-all-start.1 = ((bf16[32,2,32,256]{3,2,1,0:T(8,128)(2,1)}), bf16[32,2,32,256]{3,2,1,0:T(8,128)(2,1)}, u32[]{:S(2)}, u32[]{:S(2)}) async-start(bf16[32,2,32,256]{3,2,1,0:T(8,128)(2,1)} %pick.2), calls=%async_computation.1 | async-start | bytes 2097152 | tf_op jit(solution)/shard_map/all_to_all | solution.py:280

commit v5 on v4

--- a/solution.py
+++ b/solution.py
@@ -80,13 +80,12 @@
     )(req, rows, cols)
 
 
-def prepare_kernel(pairs, live, counts_ref, rm_ref, cm_ref, bias_ref, weight_ref):
-    slot = pl.program_id(0)
+def prepare_kernel(slot, pairs, live, counts_ref, rm_ref, cm_ref, bias_ref, weight_ref):
     size, blk = counts_ref.shape[1:]
 
     @pl.when(slot < live[0])
     def _():
-        at = pl.multiple_of(pl.program_id(1) * size, size)
+        at = pl.multiple_of(pl.program_id(0) * size, size)
         col_log = jnp.log(cm_ref[pl.ds(pairs[slot, 1], 1), :].astype(F32))
         row_log = jnp.log(rm_ref[pl.ds(pairs[slot, 0], 1), pl.ds(at, size)].astype(F32)) - LOG_TOTAL
         row_log = jnp.transpose(jnp.broadcast_to(row_log, (8, size)))[:, :1]
@@ -98,27 +97,75 @@
         weight_ref[0] = jnp.where(counts > 0.0, weight, 0.0)
 
 
-def prepare(pairs, live, counts, row_marginal, col_marginal):
-    slots, blk, _ = counts.shape
+def prepare(pairs, live, counts, row_marginal, col_marginal, slot):
+    _, blk, _ = counts.shape
     size = blk // 4
-    tile = pl.BlockSpec((1, size, blk), lambda s, i, *_: (s, i, 0))
-    whole = pl.BlockSpec(row_marginal.shape, lambda s, i, *_: (0, 0))
-    shape = jax.ShapeDtypeStruct(counts.shape, F32)
+    tile = pl.BlockSpec((1, size, blk), lambda i, *_: (slot, i, 0))
+    ready = pl.BlockSpec((1, size, blk), lambda i, *_: (0, i, 0))
+    whole = pl.BlockSpec(row_marginal.shape, lambda i, *_: (0, 0))
+    shape = jax.ShapeDtypeStruct((1, blk, blk), F32)
     return pl.pallas_call(
-        prepare_kernel,
+        functools.partial(prepare_kernel, slot),
         out_shape=(shape, shape),
         grid_spec=pltpu.PrefetchScalarGridSpec(
             num_scalar_prefetch=2,
-            grid=(slots, blk // size),
+            grid=(blk // size,),
             in_specs=[tile, whole, whole],
-            out_specs=(tile, tile),
+            out_specs=(ready, ready),
         ),
         compiler_params=params(),
         cost_estimate=pl.CostEstimate(
-            flops=10 * counts.size, bytes_accessed=12 * counts.size, transcendentals=2 * counts.size
+            flops=10 * blk * blk, bytes_accessed=12 * blk * blk, transcendentals=2 * blk * blk
         ),
         name="prepare",
     )(pairs, live, counts, row_marginal, col_marginal)
+
+
+def early_kernel(first, pairs, live, rows_ref, cols_ref, *refs):
+    *count_refs, rm_ref, cm_ref, out_ref = refs
+    slot = first + pl.program_id(0)
+    groups, _, piece, width = rows_ref.shape
+    blk = groups * piece
+    alive = slot < live[0]
+
+    @pl.when(alive)
+    def _():
+        a = pairs[slot, 0]
+        b = pairs[slot, 1]
+        cols = cols_ref[...].reshape(blk, width)
+        col_log = jnp.log(cm_ref[pl.ds(b, 1), :].astype(F32))
+        scale = 1.0 / (blk**0.5)
+        parts = []
+        deltas = []
+        for start, counts_ref in zip(range(0, blk, JOINED), count_refs):
+            span = slice(start // piece, (start + JOINED) // piece)
+            rows = rows_ref[span].reshape(JOINED, width)
+            logits = lax.dot_general(
+                rows, cols, (((1,), (1,)), ((), ())), preferred_element_type=F32
+            )
+            row_log = jnp.log(rm_ref[pl.ds(a, 1), start : start + JOINED].astype(F32)) - LOG_TOTAL
+            row_log = jnp.transpose(jnp.broadcast_to(row_log, (8, JOINED)))[:, :1]
+            counts = counts_ref[0].astype(F32)
+            seen = jnp.maximum(counts, 1.0)
+            spread = ((logits + row_log) + col_log) - jnp.log(seen)
+            weight = 0.1 * scale + (0.25 * scale) * (seen * lax.rsqrt(seen))
+            unseen = (0.5 * scale) * jnp.tanh(0.5 * spread) + 0.5 * scale
+            delta = jnp.where(counts > 0.0, weight * spread, unseen).astype(BF16)
+            row_part = jnp.dot(delta, cols, preferred_element_type=F32).astype(BF16)
+            out_ref[span, 0] = row_part.reshape(JOINED // piece, piece, width)
+            parts.append(rows)
+            deltas.append(delta)
+        col_part = lax.dot_general(
+            jnp.concatenate(parts, 0),
+            jnp.concatenate(deltas, 0),
+            (((0,), (0,)), ((), ())),
+            preferred_element_type=F32,
+        )
+        out_ref[:, 1] = jnp.transpose(col_part).astype(BF16).reshape(groups, piece, width)
+
+    @pl.when(jnp.logical_not(alive))
+    def _():
+        out_ref[...] = jnp.zeros_like(out_ref)
 
 
 def item_kernel(first, live, rows_ref, cols_ref, bias_ref, weight_ref, *refs):
@@ -174,9 +221,50 @@
     return out.transpose(1, 0, 2, 3)
 
 
+def early_items(pairs, live, got, counts, row_marginal, col_marginal, first, count):
+    width = got.shape[3]
+    blk = counts.shape[1]
+    got = join(got)
+    groups, lists, rows_in, _ = got.shape
+    whole = pl.BlockSpec(row_marginal.shape, lambda s, *_: (0, 0))
+    tiles = blk // JOINED
+
+    def table(k):
+        return pl.BlockSpec((groups, 1, rows_in, width), lambda s, *_: (0, 2 * s + k, 0, 0))
+
+    def chunk(i):
+        return pl.BlockSpec((1, JOINED, blk), lambda s, *_: (first + s, i, 0))
+
+    out = pl.pallas_call(
+        functools.partial(early_kernel, first),
+        out_shape=jax.ShapeDtypeStruct((groups, 2 * counts.shape[0], rows_in, width), BF16),
+        grid_spec=pltpu.PrefetchScalarGridSpec(
+            num_scalar_prefetch=2,
+            grid=(count,),
+            in_specs=[
+                table(0),
+                table(1),
+                *(chunk(i) for i in range(tiles)),
+                whole,
+                whole,
+            ],
+            out_specs=pl.BlockSpec((groups, 2, rows_in, width), lambda s, *_: (0, s, 0, 0)),
+        ),
+        compiler_params=params(),
+        cost_estimate=pl.CostEstimate(
+            flops=6 * count * blk * blk * width,
+            bytes_accessed=count * (blk * blk * 4 + 4 * blk * width * 2),
+            transcendentals=3 * count * blk * blk,
+        ),
+        name="early_items",
+    )(pairs, live, got, got, *([counts] * tiles), row_marginal, col_marginal)
+    return out
+
+
 def items(live, got, bias, weight, first, count, into=None):
     width = got.shape[3]
-    slots, blk, _ = bias.shape
+    blk = bias.shape[1]
+    slots = first + count
     got = join(got)
     groups, _, rows_in, _ = got.shape
     steps = blk // TILE
@@ -185,7 +273,7 @@
     def table(k):
         return pl.BlockSpec((groups, 1, rows_in, width), lambda s, i, *_: (0, 2 * s + k, 0, 0))
 
-    tile = pl.BlockSpec((1, TILE, blk), lambda s, i, *_: (first + s, i, 0))
+    tile = pl.BlockSpec((1, TILE, blk), lambda s, i, *_: (s, i, 0))
     earlier = () if into is None else (into,)
     return pl.pallas_call(
         functools.partial(item_kernel, first),
@@ -208,35 +296,24 @@
     )(live, got, got, bias, weight, *earlier)
 
 
-def update_kernel(req, ret_hbm, rm, ra, cm, ca, rn, ran, cn, can, ret_ref, grads, held, done, ret_sems, sems, out_sems):
-    lists = ret_hbm.shape[1]
+def update_kernel(req, ret_ref, rm, ra, cm, ca, rn, ran, cn, can, grads, done, out_sems):
+    nodes, lists = ret_ref.shape[:2]
     tables = ((rm, ra, rn, ran), (cm, ca, cn, can))
-    parts, loads, stores = {}, {}, []
-    for side, refs in enumerate(tables):
-        for k in range(side, lists, 2):
-            parts[k] = pltpu.make_async_copy(ret_hbm.at[:, k], ret_ref.at[k], ret_sems.at[k])
-            parts[k].start()
-        for i in range(2):
-            at = 2 * side + i
-            loads[at] = pltpu.make_async_copy(refs[i], held.at[at], sems.at[at])
-            loads[at].start()
+    stores = []
     grads[...] = jnp.zeros_like(grads)
     for side, refs in enumerate(tables):
         for k in range(side, lists, 2):
-            parts[k].wait()
 
             def one(node, carry, k=k, side=side):
-                grads[side, req[node, side, k // 2]] += ret_ref[k, node].astype(F32)
+                grads[side, req[node, side, k // 2]] += ret_ref[node, k].astype(F32)
                 return carry
 
-            lax.fori_loop(0, ret_hbm.shape[0], one, 0, unroll=4)
+            lax.fori_loop(0, nodes, one, 0, unroll=4)
         at = 2 * side
-        loads[at].wait()
-        loads[at + 1].wait()
         grad = grads[side]
-        accum_new = held[at + 1] + grad * grad
+        accum_new = refs[1][...] + grad * grad
         done[at + 1] = accum_new
-        done[at] = held[at] - LEARN_RATE * grad * lax.rsqrt(accum_new)
+        done[at] = refs[0][...] - LEARN_RATE * grad * lax.rsqrt(accum_new)
         for i in range(2):
             copy = pltpu.make_async_copy(done.at[at + i], refs[2 + i], out_sems.at[at + i])
             copy.start()
@@ -247,26 +324,21 @@
 
 def update(req, ret, row_master, row_accum, col_master, col_accum):
     shape = jax.ShapeDtypeStruct(row_master.shape, F32)
-    nodes, lists = ret.shape[:2]
     return pl.pallas_call(
         update_kernel,
         out_shape=(shape,) * 4,
         grid_spec=pltpu.PrefetchScalarGridSpec(
             num_scalar_prefetch=1,
             grid=(),
-            in_specs=[hbm_spec()] * 5,
+            in_specs=[vmem_spec()] * 5,
             out_specs=(hbm_spec(),) * 4,
             scratch_shapes=[
-                pltpu.VMEM((lists, nodes) + ret.shape[2:], BF16),
                 pltpu.VMEM((2,) + row_master.shape, F32),
                 pltpu.VMEM((4,) + row_master.shape, F32),
-                pltpu.VMEM((4,) + row_master.shape, F32),
-                pltpu.SemaphoreType.DMA((lists,)),
-                pltpu.SemaphoreType.DMA((4,)),
                 pltpu.SemaphoreType.DMA((4,)),
             ],
         ),
-        compiler_params=params(),
+        compiler_params=pltpu.CompilerParams(vmem_limit_bytes=VMEM_LIMIT // 4),
         cost_estimate=pl.CostEstimate(
             flops=8 * row_master.size + ret.size,
             bytes_accessed=ret.size * 2 + 32 * row_master.size,
@@ -290,11 +362,11 @@
     col_low = col_master.astype(BF16)
     last = slots - 1
     first_got = exchange(pick(req, row_low, col_low, 0, last))
-    bias, weight = prepare(pairs, live, counts, row_marginal, col_marginal)
+    bias, weight = prepare(pairs, live, counts, row_marginal, col_marginal, last)
     picked = pick(req, row_low, col_low, last, 1)
     picked, bias, weight = lax.optimization_barrier((picked, bias, weight))
     last_got = exchange(picked)
-    parts = items(live, first_got, bias, weight, 0, last)
+    parts = early_items(pairs, live, first_got, counts, row_marginal, col_marginal, 0, last)
     parts = items(live, last_got, bias, weight, last, 1, parts)
     back = exchange(cut(parts, nodes, row_master.shape[1]))
     return update(req, back, row_master, row_accum, col_master, col_accum)

time: 190 us -> 188 us (0.989)
  Pallas kernels: 47.5 us -> 35.8 us
  waiting for transfers between devices: 45.5 us -> 55.2 us
    pallas_call x2 -> x1, Pallas kernels: 17.3 us -> 6.31 us  [items(): pl.pallas_call(functools.partial(item_kernel, first), out_shape=jax.Shape...]
    all_to_all x3, waiting for transfers between devices: 45.5 us -> 55.2 us  [exchange(): return lax.all_to_all(x, AXES, split_axis=0, concat_axis=0, tiled=True)]
    pallas_call x1, Pallas kernels: 6.05 us -> 4.13 us  [update(): pl.pallas_call(update_kernel, out_shape=(shape,) * 4, grid_spec=pltpu.Pre...]
    pallas_call x1 -> x2, Pallas kernels: 18.1 us -> 19.4 us  [the longest x1 11.8 us: early_items(): pl.pallas_call(functools.partial(early_kernel, first), out_shape=jax.Shap...]
  transfers between devices with their start and end apart: 3 -> 3, of which waited for: 3 -> 3; matrix products, arithmetic and copies ran while one was open for 2% -> 2% of each run, Pallas kernels for 17% -> 12%
where the time goes in v5:
time: 188 us; the launch traced here: 187 us
  blocking collectives  74.5 us (40%)
  waiting for transfers between devices  55.2 us (29%)
  Pallas kernels  35.8 us (19%)
  starting transfers between devices  14.9 us (8%)
  other arithmetic  2.78 us (1%)
  local copies, waits for them, and re-layouts  2.02 us (1%)
    all_to_all x1, blocking collectives, exchange(): return lax.all_to_all(x, AXES, split_axis=0, concat_axis=0, tiled=True)  74.5 us
    all_to_all x3, waiting for transfers between devices, exchange(): return lax.all_to_all(x, AXES, split_axis=0, concat_axis=0, tiled=True)  55.2 us
    all_to_all x3, starting transfers between devices, exchange(): return lax.all_to_all(x, AXES, split_axis=0, concat_axis=0, tiled=True)  14.9 us
    pallas_call x1, Pallas kernels, early_items(): pl.pallas_call(functools.partial(early_kernel, first), out_shape=jax.Shap...  11.8 us
    pallas_call x1, Pallas kernels, prepare(): pl.pallas_call(functools.partial(prepare_kernel, slot), out_shape=(shape,...  7.56 us
    pallas_call x1, Pallas kernels, items(): pl.pallas_call(functools.partial(item_kernel, first), out_shape=jax.Shape...  6.31 us
    pallas_call x2, Pallas kernels, pick(): pl.pallas_call(functools.partial(pick_kernel, first), out_shape=jax.Shape...  5.98 us
    pallas_call x1, Pallas kernels, update(): pl.pallas_call(update_kernel, out_shape=(shape,) * 4, grid_spec=pltpu.Pre...  4.13 us
  transfers between devices with their start and end apart: 3, of which 3 were waited for; matrix products, arithmetic and copies ran while one was open for 2% of the time, Pallas kernels for 12%

profile of v5, /device:TPU:0, one launch (start us, length us, event | category | flops | bytes accessed | tf_op | source)
XLA Modules:
  0.0 186.6 jit_solution(12648836557616958569)
XLA Ops:
  0.6 1.3 broadcast_in_dim.2
  1.9 7.3 %all-to-all-start = ((s32[32,2,3]{2,1,0:T(2,128)}), s32[32,2,3]{2,1,0:T(2,128)S(1)}, u32[]{:S(2)}, u32[]{:S(2)}) async-start(s32[32,2,3]{2,1,0:T(2,128)} %broadcast_in_dim.2), calls=%async_computation | async-start | bytes 65536 | tf_op jit(solution)/shard_map/all_to_all | solution.py:352
  9.2 1.3 convert_element_type.6.row_ref
  10.5 0.0 copy-start
  10.6 1.5 convert_element_type.7.col_ref
  12.1 0.0 copy-start.1
  12.1 0.0 copy-start.8
  12.1 4.4 %all-to-all-done.req = s32[32,2,3]{2,1,0:T(2,128)S(1)} async-done(((s32[32,2,3]{2,1,0:T(2,128)}), s32[32,2,3]{2,1,0:T(2,128)S(1)}, u32[]{:S(2)}, u32[]{:S(2)}) %all-to-all-start) | async-done | bytes 800 | tf_op jit(solution)/shard_map/all_to_all | solution.py:352
  16.5 2.6 %pick.3 = bf16[32,4,32,256]{3,2,1,0:T(8,128)(2,1)} custom-call(s32[32,2,3]{2,1,0:T(2,128)S(1)} %all-to-all-done.req, bf16[32,32,256]{2,1,0:T(8,128)(2,1)S(1)} %convert_element_type.6.row_ref, bf16[32,32,256]{2,1,0:T(8,128)(2,1)S(1)} %convert_element_type.7.col_ref), custom_call_target="tpu_custom_call" | custom-call | bytes 3145728 | tf_op jit(solution)/shard_map/pick/pallas_call | solution.py:60
  19.0 0.0 copy-done
  19.1 0.0 copy-done.1
  19.1 3.5 %all-to-all-start.2 = ((bf16[32,4,32,256]{3,2,1,0:T(8,128)(2,1)}), bf16[32,4,32,256]{3,2,1,0:T(8,128)(2,1)}, u32[]{:S(2)}, u32[]{:S(2)}) async-start(bf16[32,4,32,256]{3,2,1,0:T(8,128)(2,1)} %pick.3), calls=%async_computation.2 | async-start | bytes 4194304 | tf_op jit(solution)/shard_map/all_to_all | solution.py:352
  22.6 0.7 copy.14.pairs
  23.9 7.6 %prepare.1 = (f32[1,1024,1024]{2,1,0:T(8,128)}, f32[1,1024,1024]{2,1,0:T(8,128)}) custom-call(s32[3,2]{1,0:T(4,128)} %copy.14.pairs, s32[1]{0:T(128)S(6)} %copy.17.live, s32[3,1024,1024]{2,1,0:T(8,128)} %refs_3_.1, s32[32,1024]{1,0:T(8,128)} %refs_4_.1, s32[32,1024]{1,0:T(8,128)} %refs_5_.1), custom_call_target="tpu_custom_call" | custom-call | flops 10485760 | bytes 12582912 | tf_op jit(solution)/shard_map/prepare/pallas_call | solution.py:107
  31.5 3.4 %pick.2 = bf16[32,2,32,256]{3,2,1,0:T(8,128)(2,1)} custom-call(s32[32,2,3]{2,1,0:T(2,128)} %copy-done.6, bf16[32,32,256]{2,1,0:T(8,128)(2,1)} %copy-done, bf16[32,32,256]{2,1,0:T(8,128)(2,1)} %copy-done.1), custom_call_target="tpu_custom_call" | custom-call | bytes 2097152 | tf_op jit(solution)/shard_map/pick/pallas_call | solution.py:60
  34.9 36.4 %all-to-all-done.2.rows_ref.cols_ref = bf16[32,4,32,256]{3,2,1,0:T(8,128)(2,1)} async-done(((bf16[32,4,32,256]{3,2,1,0:T(8,128)(2,1)}), bf16[32,4,32,256]{3,2,1,0:T(8,128)(2,1)}, u32[]{:S(2)}, u32[]{:S(2)}) %all-to-all-start.2) | async-done | bytes 2097184 | tf_op jit(solution)/shard_map/all_to_all | solution.py:352
  71.3 4.1 %all-to-all-start.1 = ((bf16[32,2,32,256]{3,2,1,0:T(8,128)(2,1)}), bf16[32,2,32,256]{3,2,1,0:T(8,128)(2,1)}, u32[]{:S(2)}, u32[]{:S(2)}) async-start(bf16[32,2,32,256]{3,2,1,0:T(8,128)(2,1)} %pick.2), calls=%async_computation.1 | async-start | bytes 2097152 | tf_op jit(solution)/shard_map/all_to_all | solution.py:352
  75.4 11.8 %early_items.1.refs_0_ = bf16[32,6,32,256]{3,2,1,0:T(8,128)(2,1)} custom-call(s32[3,2]{1,0:T(4,128)} %copy.14.pairs, s32[1]{0:T(128)S(6)} %copy.17.live, bf16[32,4,32,256]{3,2,1,0:T(8,128)(2,1)} %all-to-all-done.2.rows_ref.cols_ref, bf16[32,4,32,256]{3,2,1,0:T(8,128)(2,1)} %all-to-all-done.2.rows_ref.cols_ref, s32[3,1024,1024]{2,1,0:T(8,128)} %refs_3_.1, ...), custom_call_target="tpu_custom_call" | custom-call | flops 3221225472 | bytes 12582912 | tf_op jit(solution)/shard_map/early_items/pallas_call | solution.py:238
  87.2 14.4 %all-to-all-done.1.rows_ref.cols_ref = bf16[32,2,32,256]{3,2,1,0:T(8,128)(2,1)} async-done(((bf16[32,2,32,256]{3,2,1,0:T(8,128)(2,1)}), bf16[32,2,32,256]{3,2,1,0:T(8,128)(2,1)}, u32[]{:S(2)}, u32[]{:S(2)}) %all-to-all-start.1) | async-done | bytes 1048608 | tf_op jit(solution)/shard_map/all_to_all | solution.py:352
  101.6 6.3 %items.1 = bf16[32,6,32,256]{3,2,1,0:T(8,128)(2,1)} custom-call(s32[1]{0:T(128)S(6)} %copy.17.live, bf16[32,2,32,256]{3,2,1,0:T(8,128)(2,1)} %all-to-all-done.1.rows_ref.cols_ref, bf16[32,2,32,256]{3,2,1,0:T(8,128)(2,1)} %all-to-all-done.1.rows_ref.cols_ref, f32[1,1024,1024]{2,1,0:T(8,128)} %get-tuple-element.12.bias_ref, ...), custom_call_target="tpu_custom_call", output_to_operand_aliasing={{}: (5, {})} | custom-call | flops 1610612736 | bytes 10485760 | tf_op jit(solution)/shard_map/items/pallas_call | solution.py:278
  108.0 0.0 copy-start.5
  108.0 0.0 copy-start.7
  108.0 74.5 %all_to_all.20.ret_ref = bf16[32,6,32,256]{3,2,1,0:T(8,128)(2,1)S(1)} all-to-all(bf16[32,6,32,256]{3,2,1,0:T(8,128)(2,1)} %items.1), channel_id=1, replica_groups=mesh['rows'=8,'cols'=4] {'rows','cols'}, dimensions={0} | all-to-all | bytes 6291456 | tf_op jit(solution)/shard_map/all_to_all | solution.py:352
  182.5 4.1 %update.1 = (f32[32,32,256]{2,1,0:T(8,128)}, f32[32,32,256]{2,1,0:T(8,128)}, f32[32,32,256]{2,1,0:T(8,128)}, f32[32,32,256]{2,1,0:T(8,128)}) custom-call(s32[32,2,3]{2,1,0:T(2,128)S(1)} %copy-done.7, bf16[32,6,32,256]{3,2,1,0:T(8,128)(2,1)S(1)} %all_to_all.20.ret_ref, f32[32,32,256]{2,1,0:T(8,128)S(1)} %copy-done.2, f32[32,32,256]{2,1,0:T(8,128)S(1)} %copy-done.4, ...), custom_call_target="tpu_custom_call" | custom-call | flops 3670016 | bytes 11534336 | tf_op jit(solution)/shard_map/update/pallas_call | solution.py:327
  (11 shorter events, 0.0 us)
Async XLA Ops:
  1.9 14.6 %all-to-all-start = ((s32[32,2,3]{2,1,0:T(2,128)}), s32[32,2,3]{2,1,0:T(2,128)S(1)}, u32[]{:S(2)}, u32[]{:S(2)}) async-start(s32[32,2,3]{2,1,0:T(2,128)} %broadcast_in_dim.2), calls=%async_computation | async-start | bytes 65536 | tf_op jit(solution)/shard_map/all_to_all | solution.py:352
  10.5 8.5 %copy-start = (bf16[32,32,256]{2,1,0:T(8,128)(2,1)}, bf16[32,32,256]{2,1,0:T(8,128)(2,1)S(1)}, u32[]{:S(2)}) copy-start(bf16[32,32,256]{2,1,0:T(8,128)(2,1)S(1)} %convert_element_type.6.row_ref) | copy-start | bytes 1572868
  12.1 7.0 %copy-start.1 = (bf16[32,32,256]{2,1,0:T(8,128)(2,1)}, bf16[32,32,256]{2,1,0:T(8,128)(2,1)S(1)}, u32[]{:S(2)}) copy-start(bf16[32,32,256]{2,1,0:T(8,128)(2,1)S(1)} %convert_element_type.7.col_ref) | copy-start | bytes 1572868
  12.1 10.5 %copy-start.8 = (s32[3,2]{0,1:T(2,128)S(1)}, s32[3,2]{0,1:T(2,128)}, u32[]{:S(2)}) copy-start(s32[3,2]{0,1:T(2,128)} %param.13) | copy-start | bytes 76
  16.5 2.6 %copy-start.6 = (s32[32,2,3]{2,1,0:T(2,128)}, s32[32,2,3]{2,1,0:T(2,128)S(1)}, u32[]{:S(2)}) copy-start(s32[32,2,3]{2,1,0:T(2,128)S(1)} %all-to-all-done.req) | copy-start | bytes 2308
  19.1 52.2 %all-to-all-start.2 = ((bf16[32,4,32,256]{3,2,1,0:T(8,128)(2,1)}), bf16[32,4,32,256]{3,2,1,0:T(8,128)(2,1)}, u32[]{:S(2)}, u32[]{:S(2)}) async-start(bf16[32,4,32,256]{3,2,1,0:T(8,128)(2,1)} %pick.3), calls=%async_computation.2 | async-start | bytes 4194304 | tf_op jit(solution)/shard_map/all_to_all | solution.py:352
  71.3 30.3 %all-to-all-start.1 = ((bf16[32,2,32,256]{3,2,1,0:T(8,128)(2,1)}), bf16[32,2,32,256]{3,2,1,0:T(8,128)(2,1)}, u32[]{:S(2)}, u32[]{:S(2)}) async-start(bf16[32,2,32,256]{3,2,1,0:T(8,128)(2,1)} %pick.2), calls=%async_computation.1 | async-start | bytes 2097152 | tf_op jit(solution)/shard_map/all_to_all | solution.py:352
  107.9 74.5 %copy-start.2 = (f32[32,32,256]{2,1,0:T(8,128)S(1)}, f32[32,32,256]{2,1,0:T(8,128)}, u32[]{:S(2)}) copy-start(f32[32,32,256]{2,1,0:T(8,128)} %rm.1) | copy-start | bytes 3145732
  107.9 74.5 %copy-start.3 = (f32[32,32,256]{2,1,0:T(8,128)S(1)}, f32[32,32,256]{2,1,0:T(8,128)}, u32[]{:S(2)}) copy-start(f32[32,32,256]{2,1,0:T(8,128)} %cm.1) | copy-start | bytes 3145732
  107.9 74.5 %copy-start.4 = (f32[32,32,256]{2,1,0:T(8,128)S(1)}, f32[32,32,256]{2,1,0:T(8,128)}, u32[]{:S(2)}) copy-start(f32[32,32,256]{2,1,0:T(8,128)} %ra.1) | copy-start | bytes 3145732
  108.0 74.5 %copy-start.5 = (f32[32,32,256]{2,1,0:T(8,128)S(1)}, f32[32,32,256]{2,1,0:T(8,128)}, u32[]{:S(2)}) copy-start(f32[32,32,256]{2,1,0:T(8,128)} %ca.1) | copy-start | bytes 3145732
  108.0 74.5 %copy-start.7 = (s32[32,2,3]{2,1,0:T(2,128)S(1)}, s32[32,2,3]{2,1,0:T(2,128)}, u32[]{:S(2)}) copy-start(s32[32,2,3]{2,1,0:T(2,128)} %copy-done.6) | copy-start | bytes 2308

commit v6 on v3

v6 whole, which is shorter than its diff:
```python
import functools

import jax
import jax.numpy as jnp
from jax import lax
from jax.experimental import pallas as pl
from jax.experimental.pallas import tpu as pltpu
from jax.sharding import PartitionSpec as P

LOG_TOTAL = 14.3
LEARN_RATE = 0.05
AXES = ("rows", "cols")
TILE = 512
JOINED = 256
VMEM_LIMIT = 65280 * 1024

BF16 = jnp.bfloat16
F32 = jnp.float32


def vmem_spec():
    return pl.BlockSpec(memory_space=pltpu.VMEM)


def hbm_spec():
    return pl.BlockSpec(memory_space=pltpu.HBM)


def params():
    return pltpu.CompilerParams(vmem_limit_bytes=VMEM_LIMIT)


def pick_kernel(first, req, pairs, live, row_ref, col_ref, out_ref, held, sems):
    nodes, lists = out_ref.shape[:2]
    chunks = sems.shape[0]
    span = nodes // chunks
    copies = []
    for chunk in range(chunks):

        def one(i, carry, base=chunk * span):
            node = base + i
            for k in range(0, lists, 2):
                held[node, k] = row_ref[req[node, 0, first + k // 2]]
                held[node, k + 1] = col_ref[req[node, 1, first + k // 2]]
            return carry

        lax.fori_loop(0, span, one, 0)
        part = pl.ds(chunk * span, span)
        copy = pltpu.make_async_copy(held.at[part], out_ref.at[part], sems.at[chunk])
        copy.start()
        copies.append(copy)
    for copy in copies:
        copy.wait()


def pick(req, pairs, live, rows, cols, first, count):
    nodes = req.shape[0]
    lists = 2 * count
    piece, width = rows.shape[1:]
    return pl.pallas_call(
        functools.partial(pick_kernel, first),
        out_shape=jax.ShapeDtypeStruct((nodes, lists, piece, width), BF16),
        grid_spec=pltpu.PrefetchScalarGridSpec(
            num_scalar_prefetch=3,
            grid=(),
            in_specs=[vmem_spec()] * 2,
            out_specs=hbm_spec(),
            scratch_shapes=[
                pltpu.VMEM((nodes, lists, piece, width), BF16),
                pltpu.SemaphoreType.DMA((8,)),
            ],
        ),
        compiler_params=pltpu.CompilerParams(vmem_limit_bytes=VMEM_LIMIT if first else VMEM_LIMIT // 4),
        cost_estimate=pl.CostEstimate(
            flops=0,
            bytes_accessed=4 * rows.size + nodes * lists * piece * width * 2,
            transcendentals=0,
        ),
        name="pick",
    )(req, pairs, live, rows, cols)


def item_kernel(pairs, live, got_ref, *refs):
    *count_refs, rm_ref, cm_ref, out_ref = refs
    slot = pl.program_id(0)
    groups, _, piece, width = got_ref.shape
    blk = groups * piece
    alive = slot < live[0]

    @pl.when(alive)
    def _():
        a = pairs[slot, 0]
        b = pairs[slot, 1]
        cols = got_ref[:, 2 * slot + 1].reshape(blk, width)
        col_log = jnp.log(cm_ref[pl.ds(b, 1), :].astype(F32))
        scale = 1.0 / (blk**0.5)
        parts = []
        deltas = []
        for start, counts_ref in zip(range(0, blk, TILE), count_refs):
            span = slice(start // piece, (start + TILE) // piece)
            rows = got_ref[span, 2 * slot].reshape(TILE, width)
            logits = lax.dot_general(
                rows, cols, (((1,), (1,)), ((), ())), preferred_element_type=F32
            )
            row_log = jnp.log(rm_ref[pl.ds(a, 1), start : start + TILE].astype(F32)) - LOG_TOTAL
            row_log = jnp.transpose(jnp.broadcast_to(row_log, (8, TILE)))[:, :1]
            counts = counts_ref[0].astype(F32)
            seen = jnp.maximum(counts, 1.0)
            spread = ((logits + row_log) + col_log) - jnp.log(seen)
            weight = 0.1 * scale + (0.25 * scale) * (seen * lax.rsqrt(seen))
            unseen = (0.5 * scale) * jnp.tanh(0.5 * spread) + 0.5 * scale
            delta = jnp.where(counts > 0.0, weight * spread, unseen).astype(BF16)
            row_part = jnp.dot(delta, cols, preferred_element_type=F32).astype(BF16)
            out_ref[span, 2 * slot] = row_part.reshape(TILE // piece, piece, width)
            parts.append(rows)
            deltas.append(delta)
        col_part = lax.dot_general(
            jnp.concatenate(parts, 0),
            jnp.concatenate(deltas, 0),
            (((0,), (0,)), ((), ())),
            preferred_element_type=F32,
        )
        out_ref[:, 2 * slot + 1] = jnp.transpose(col_part).astype(BF16).reshape(groups, piece, width)

    @pl.when(jnp.logical_not(alive))
    def _():
        for side in range(2):
            out_ref[:, 2 * slot + side] = jnp.zeros((groups, piece, width), BF16)


def join(got):
    nodes, lists, piece, width = got.shape
    if piece % 16 == 0:
        return got
    got = got.transpose(1, 0, 2, 3).reshape(lists, nodes * piece // JOINED, JOINED, width)
    return got.transpose(1, 0, 2, 3)


def cut(out, nodes, piece):
    groups, lists, rows, width = out.shape
    if rows == piece:
        return out
    out = out.transpose(1, 0, 2, 3).reshape(lists, nodes, piece, width)
    return out.transpose(1, 0, 2, 3)


def items(pairs, live, got, counts, row_marginal, col_marginal):
    nodes, _, piece, width = got.shape
    count, blk, _ = counts.shape
    got = join(got)
    tiles = blk // TILE

    def chunk(i):
        return pl.BlockSpec((1, TILE, blk), lambda s, *_: (s, i, 0))

    out = pl.pallas_call(
        item_kernel,
        out_shape=jax.ShapeDtypeStruct(got.shape, BF16),
        grid_spec=pltpu.PrefetchScalarGridSpec(
            num_scalar_prefetch=2,
            grid=(count,),
            in_specs=[vmem_spec(), *(chunk(i) for i in range(tiles)), vmem_spec(), vmem_spec()],
            out_specs=vmem_spec(),
        ),
        compiler_params=pltpu.CompilerParams(vmem_limit_bytes=VMEM_LIMIT * 5 // 8),
        cost_estimate=pl.CostEstimate(
            flops=6 * count * blk * blk * width,
            bytes_accessed=count * (blk * blk * 4 + 4 * blk * width * 2),
            transcendentals=3 * count * blk * blk,
        ),
        name="items",
    )(pairs, live, got, *([counts] * tiles), row_marginal, col_marginal)
    return cut(out, nodes, piece)


def update_kernel(req, ret_ref, rm, ra, cm, ca, rn, ran, cn, can, grads, done, out_sems):
    nodes, lists = ret_ref.shape[:2]
    tables = ((rm, ra, rn, ran), (cm, ca, cn, can))
    stores = []
    grads[...] = jnp.zeros_like(grads)
    for side, refs in enumerate(tables):
        for k in range(side, lists, 2):

            def one(node, carry, k=k, side=side):
                grads[side, req[node, side, k // 2]] += ret_ref[node, k].astype(F32)
                return carry

            lax.fori_loop(0, nodes, one, 0, unroll=4)
        at = 2 * side
        grad = grads[side]
        accum_new = refs[1][...] + grad * grad
        done[at + 1] = accum_new
        done[at] = refs[0][...] - LEARN_RATE * grad * lax.rsqrt(accum_new)
        for i in range(2):
            copy = pltpu.make_async_copy(done.at[at + i], refs[2 + i], out_sems.at[at + i])
            copy.start()
            stores.append(copy)
    for copy in stores:
        copy.wait()


def update(req, ret, row_master, row_accum, col_master, col_accum):
    shape = jax.ShapeDtypeStruct(row_master.shape, F32)
    return pl.pallas_call(
        update_kernel,
        out_shape=(shape,) * 4,
        grid_spec=pltpu.PrefetchScalarGridSpec(
            num_scalar_prefetch=1,
            grid=(),
            in_specs=[vmem_spec()] * 5,
            out_specs=(hbm_spec(),) * 4,
            scratch_shapes=[
                pltpu.VMEM((2,) + row_master.shape, F32),
                pltpu.VMEM((4,) + row_master.shape, F32),
                pltpu.SemaphoreType.DMA((4,)),
            ],
        ),
        compiler_params=pltpu.CompilerParams(vmem_limit_bytes=VMEM_LIMIT // 4),
        cost_estimate=pl.CostEstimate(
            flops=8 * row_master.size + ret.size,
            bytes_accessed=ret.size * 2 + 32 * row_master.size,
            transcendentals=2 * row_master.size,
        ),
        name="update",
    )(req, ret, row_master, row_accum, col_master, col_accum)


def exchange(x):
    return lax.all_to_all(x, AXES, split_axis=0, concat_axis=0, tiled=True)


def body(
    row_master, row_accum, col_master, col_accum, pairs, live, counts, row_marginal, col_marginal
):
    slots = pairs.shape[0]
    nodes = lax.axis_size(AXES)
    req = exchange(jnp.broadcast_to(pairs.T[None], (nodes, 2, slots)))
    row_low = row_master.astype(BF16)
    col_low = col_master.astype(BF16)
    got = exchange(pick(req, pairs, live, row_low, col_low, 0, slots))
    back = exchange(items(pairs, live, got, counts, row_marginal, col_marginal))
    return update(req, back, row_master, row_accum, col_master, col_accum)


def solution(mesh):
    table = P(None, AXES, None)
    return jax.shard_map(
        body,
        mesh=mesh,
        in_specs=(
            table,
            table,
            table,
            table,
            P(AXES, None),
            P(AXES),
            P(AXES, None, None),
            P(),
            P(),
        ),
        out_specs=(table,) * 4,
        check_vma=False,
    )
```

time: 191 us -> 186 us (0.974)
  blocking collectives: 0 us -> 148 us
  waiting for transfers between devices: 129 us -> 3.22 us
  starting transfers between devices: 22.9 us -> 7.3 us
  Pallas kernels: 34.1 us -> 20.8 us
    all_to_all x0 -> x2, blocking collectives: none -> 148 us  [exchange(): return lax.all_to_all(x, AXES, split_axis=0, concat_axis=0, tiled=True)]
    all_to_all x5 -> x1, waiting for transfers between devices: 129 us -> 3.22 us  [exchange(): return lax.all_to_all(x, AXES, split_axis=0, concat_axis=0, tiled=True)]
    all_to_all x5 -> x1, starting transfers between devices: 22.9 us -> 7.3 us  [exchange(): return lax.all_to_all(x, AXES, split_axis=0, concat_axis=0, tiled=True)]
    pallas_call x4 -> x2, Pallas kernels: 30 us -> 17.8 us  [the longest x1 13.6 us: items(): pl.pallas_call(item_kernel, out_shape=jax.ShapeDtypeStruct(got.shape, BF1...]
    pallas_call x2 -> x1, Pallas kernels: 4.08 us -> 3.08 us  [pick(): pl.pallas_call(functools.partial(pick_kernel, first), out_shape=jax.Shape...]
  transfers between devices with their start and end apart: 5 -> 1, of which waited for: 5 -> 1; matrix products, arithmetic and copies ran while one was open for 1% -> 2% of each run, Pallas kernels for 14% -> 0%
where the time goes in v6:
time: 186 us
  blocking collectives  148 us (80%)
  Pallas kernels  20.8 us (11%)
  starting transfers between devices  7.3 us (4%)
  waiting for transfers between devices  3.22 us (2%)
  other arithmetic  2.6 us (1%)
  local copies, waits for them, and re-layouts  2.11 us (1%)
    all_to_all x2, blocking collectives, exchange(): return lax.all_to_all(x, AXES, split_axis=0, concat_axis=0, tiled=True)  148 us
    pallas_call x1, Pallas kernels, items(): pl.pallas_call(item_kernel, out_shape=jax.ShapeDtypeStruct(got.shape, BF1...  13.6 us
    all_to_all x1, starting transfers between devices, exchange(): return lax.all_to_all(x, AXES, split_axis=0, concat_axis=0, tiled=True)  7.3 us
    pallas_call x1, Pallas kernels, update(): pl.pallas_call(update_kernel, out_shape=(shape,) * 4, grid_spec=pltpu.Pre...  4.13 us
  transfers between devices with their start and end apart: 1, of which 1 were waited for; matrix products, arithmetic and copies ran while one was open for 2% of the time, Pallas kernels for 0%

profile of v6, /device:TPU:0, one launch (start us, length us, event | category | flops | bytes accessed | tf_op | source)
XLA Modules:
  0.0 185.7 jit_solution(6862865256712090779)
XLA Ops:
  0.6 1.3 broadcast_in_dim.2
  1.9 7.3 %all-to-all-start = ((s32[32,2,3]{2,1,0:T(2,128)}), s32[32,2,3]{2,1,0:T(2,128)S(1)}, u32[]{:S(2)}, u32[]{:S(2)}) async-start(s32[32,2,3]{2,1,0:T(2,128)} %broadcast_in_dim.2), calls=%async_computation | async-start | bytes 65536 | tf_op jit(solution)/shard_map/all_to_all | solution.py:229
  9.2 0.8 copy.14.pairs
  10.7 1.3 convert_element_type.6.row_ref
  12.0 1.3 convert_element_type.7.col_ref
  13.3 3.2 %all-to-all-done.req = s32[32,2,3]{2,1,0:T(2,128)S(1)} async-done(((s32[32,2,3]{2,1,0:T(2,128)}), s32[32,2,3]{2,1,0:T(2,128)S(1)}, u32[]{:S(2)}, u32[]{:S(2)}) %all-to-all-start) | async-done | bytes 800 | tf_op jit(solution)/shard_map/all_to_all | solution.py:229
  16.5 3.1 %pick.1 = bf16[32,6,32,256]{3,2,1,0:T(8,128)(2,1)S(1)} custom-call(s32[32,2,3]{2,1,0:T(2,128)S(1)} %all-to-all-done.req, s32[3,2]{1,0:T(4,128)S(1)} %copy.14.pairs, s32[1]{0:T(128)S(6)} %copy.15.live, bf16[32,32,256]{2,1,0:T(8,128)(2,1)S(1)} %convert_element_type.6.row_ref, bf16[32,32,256]{2,1,0:T(8,128)(2,1)S(1)} %convert_element_type.7.col_ref), custom_call_target="tpu_custom_call" | custom-call | bytes 4194304 | tf_op jit(solution)/shard_map/pick/pallas_call | solution.py:60
  19.6 0.0 copy-start.4
  19.6 0.0 copy-start.5
  19.6 73.6 %all_to_all.15.got_ref = bf16[32,6,32,256]{3,2,1,0:T(8,128)(2,1)S(1)} all-to-all(bf16[32,6,32,256]{3,2,1,0:T(8,128)(2,1)S(1)} %pick.1), channel_id=1, replica_groups=mesh['rows'=8,'cols'=4] {'rows','cols'}, dimensions={0} | all-to-all | bytes 6291456 | tf_op jit(solution)/shard_map/all_to_all | solution.py:229
  93.2 0.0 copy-done.4
  93.2 0.0 copy-done.5
  93.2 13.6 %items.1 = bf16[32,6,32,256]{3,2,1,0:T(8,128)(2,1)S(1)} custom-call(s32[3,2]{1,0:T(4,128)S(1)} %copy.14.pairs, s32[1]{0:T(128)S(6)} %copy.15.live, bf16[32,6,32,256]{3,2,1,0:T(8,128)(2,1)S(1)} %all_to_all.15.got_ref, s32[3,1024,1024]{2,1,0:T(8,128)} %refs_1_.1, s32[3,1024,1024]{2,1,0:T(8,128)} %refs_1_.1, s32[32,1024]{1,0:T(8,128)S(1)} %copy-done.4, ...), custom_call_target="tpu_custom_call" | custom-call | flops 4831838208 | bytes 18874368 | tf_op jit(solution)/shard_map/items/pallas_call | solution.py:156
  106.9 0.0 copy-start
  106.9 0.0 copy-start.1
  106.9 0.0 copy-start.2
  106.9 0.0 copy-start.3
  106.9 74.6 %all_to_all.16.ret_ref = bf16[32,6,32,256]{3,2,1,0:T(8,128)(2,1)S(1)} all-to-all(bf16[32,6,32,256]{3,2,1,0:T(8,128)(2,1)S(1)} %items.1), channel_id=1, replica_groups=mesh['rows'=8,'cols'=4] {'rows','cols'}, dimensions={0} | all-to-all | bytes 6291456 | tf_op jit(solution)/shard_map/all_to_all | solution.py:229
  181.5 0.0 copy-done
  181.5 0.0 copy-done.1
  181.5 0.0 copy-done.2
  181.5 0.0 copy-done.3
  181.6 4.1 %update.1 = (f32[32,32,256]{2,1,0:T(8,128)}, f32[32,32,256]{2,1,0:T(8,128)}, f32[32,32,256]{2,1,0:T(8,128)}, f32[32,32,256]{2,1,0:T(8,128)}) custom-call(s32[32,2,3]{2,1,0:T(2,128)S(1)} %all-to-all-done.req, bf16[32,6,32,256]{3,2,1,0:T(8,128)(2,1)S(1)} %all_to_all.16.ret_ref, f32[32,32,256]{2,1,0:T(8,128)S(1)} %copy-done, f32[32,32,256]{2,1,0:T(8,128)S(1)} %copy-done.2, ...), custom_call_target="tpu_custom_call" | custom-call | flops 3670016 | bytes 11534336 | tf_op jit(solution)/shard_map/update/pallas_call | solution.py:204
Async XLA Ops:
  1.9 14.6 %all-to-all-start = ((s32[32,2,3]{2,1,0:T(2,128)}), s32[32,2,3]{2,1,0:T(2,128)S(1)}, u32[]{:S(2)}, u32[]{:S(2)}) async-start(s32[32,2,3]{2,1,0:T(2,128)} %broadcast_in_dim.2), calls=%async_computation | async-start | bytes 65536 | tf_op jit(solution)/shard_map/all_to_all | solution.py:229
  19.6 73.6 %copy-start.4 = (s32[32,1024]{1,0:T(8,128)S(1)}, s32[32,1024]{1,0:T(8,128)}, u32[]{:S(2)}) copy-start(s32[32,1024]{1,0:T(8,128)} %refs_2_.1) | copy-start | bytes 393220
  19.6 73.6 %copy-start.5 = (s32[32,1024]{1,0:T(8,128)S(1)}, s32[32,1024]{1,0:T(8,128)}, u32[]{:S(2)}) copy-start(s32[32,1024]{1,0:T(8,128)} %refs_3_.1) | copy-start | bytes 393220
  106.9 74.7 %copy-start = (f32[32,32,256]{2,1,0:T(8,128)S(1)}, f32[32,32,256]{2,1,0:T(8,128)}, u32[]{:S(2)}) copy-start(f32[32,32,256]{2,1,0:T(8,128)} %rm.1) | copy-start | bytes 3145732
  106.9 74.7 %copy-start.1 = (f32[32,32,256]{2,1,0:T(8,128)S(1)}, f32[32,32,256]{2,1,0:T(8,128)}, u32[]{:S(2)}) copy-start(f32[32,32,256]{2,1,0:T(8,128)} %cm.1) | copy-start | bytes 3145732
  106.9 74.7 %copy-start.2 = (f32[32,32,256]{2,1,0:T(8,128)S(1)}, f32[32,32,256]{2,1,0:T(8,128)}, u32[]{:S(2)}) copy-start(f32[32,32,256]{2,1,0:T(8,128)} %ra.1) | copy-start | bytes 3145732
  106.9 74.7 %copy-start.3 = (f32[32,32,256]{2,1,0:T(8,128)S(1)}, f32[32,32,256]{2,1,0:T(8,128)}, u32[]{:S(2)}) copy-start(f32[32,32,256]{2,1,0:T(8,128)} %ca.1) | copy-start | bytes 3145732
